TPU v7x, 32 devices: a whole 2x2x4 slice. The times are simulated.
32 devices in a mesh: blk: 8 (over z, y), feat: 4 (over x, core).
Axes of the slice: x: 2, y: 2, z: 4, core: 2. Of those that a mesh axis runs over, the one named last changes fastest.
Arguments:
- image: bfloat16 [1408, 1152], P('blk', 'feat'), may hold values from -6 to 6
- text: bfloat16 [1408, 1152], P('blk', 'feat'), may hold values from -6 to 6
- scale: float32 [], replicated, may hold values from 0.05 to 0.12
- bias: float32 [], replicated, may hold values from -7 to -4
Outputs:
- image_grad: float32 [1408, 1152], P('blk', 'feat')
- text_grad: float32 [1408, 1152], P('blk', 'feat')
All inputs are finite; a program needn't handle non-finite values.
Results may differ from a plain program's by a relative error of at most 0.0013.
Values may be sent and summed in bfloat16 or wider, within the bound.
A program may use at most 64 MiB of HBM per device.

v0:
```python
import jax
import jax.numpy as jnp
from jax import lax
from jax.sharding import PartitionSpec as P


def from_behind(block, axis, distance):
    devices = range(lax.axis_size(axis))
    route = [((i - distance) % len(devices), i) for i in devices]
    return lax.ppermute(block, axis, route)


def pair_grads(image_all, current, scale, bias, diag_start, own):
    dots = lax.dot_general(
        image_all, current, (((1,), (1,)), ((), ())), preferred_element_type=jnp.float32
    )
    logit = scale * dots + bias
    if own:
        row_index = lax.broadcasted_iota(jnp.int32, logit.shape, 0)
        col_index = diag_start + lax.broadcasted_iota(jnp.int32, logit.shape, 1)
        value = jnp.where(row_index == col_index, -jax.nn.sigmoid(-logit), jax.nn.sigmoid(logit))
    else:
        value = jax.nn.sigmoid(logit)
    slope = value.astype(jnp.bfloat16)
    image_add = jnp.dot(slope, current, preferred_element_type=jnp.float32)
    text_add = lax.dot_general(
        slope, image_all, (((0,), (0,)), ((), ())), preferred_element_type=jnp.float32
    )
    return (image_add, text_add)


def pass_both(current, accum):
    return (
        from_behind(current.astype(jnp.float32), "blk", 1).astype(current.dtype),
        from_behind(accum, "blk", 1),
    )


def shards(image, text, scale, bias):
    block_count = lax.axis_size("blk")
    image_all = lax.all_gather(image, "feat", axis=1, tiled=True)
    quarter = lax.all_to_all(text, "feat", split_axis=0, concat_axis=1, tiled=True)
    rows_q = quarter.shape[0]
    diag_start = lax.axis_index("feat") * rows_q
    image_acc, text_acc = pair_grads(image_all, quarter, scale, bias, diag_start, True)

    def visit(step, carry):
        current, accum, grad_img = carry
        current, accum = pass_both(current, accum)
        image_add, text_add = pair_grads(image_all, current, scale, bias, 0, False)
        return (current, accum + text_add, grad_img + image_add)

    current, text_acc, image_acc = lax.fori_loop(
        1, block_count, visit, (quarter, text_acc, image_acc)
    )
    text_acc = from_behind(text_acc, "blk", 1)
    image_grad = scale * lax.psum_scatter(image_acc, "feat", scatter_dimension=1, tiled=True)
    text_grad = lax.all_to_all(scale * text_acc, "feat", split_axis=1, concat_axis=0, tiled=True)
    return (image_grad, text_grad)


def solution(mesh):
    in_specs = (P("blk", "feat"), P("blk", "feat"), P(), P())
    out_specs = (P("blk", "feat"), P("blk", "feat"))
    return jax.shard_map(shards, mesh=mesh, in_specs=in_specs, out_specs=out_specs, check_vma=False)
```

profile of v0, /device:TPU:0, one launch (start us, length us, event | category | flops | bytes accessed | tf_op | source)
XLA Modules:
  0.0 138.2 jit_solution(17663519637187326307)
XLA Ops:
  7.2 1.6 %all_to_all.28 = bf16[4,44,288]{2,1,0:T(8,128)(2,1)} reshape(bf16[176,288]{1,0:T(8,128)(2,1)} %param.7) | data formatting | bytes 202752 | tf_op jit(solution)/shard_map/all_to_all | solution.py:42
  8.8 4.2 %all-to-all-start = ((bf16[4,44,288]{2,1,0:T(8,128)(2,1)}), bf16[4,44,288]{2,1,0:T(8,128)(2,1)S(1)}, u32[]{:S(2)}, u32[]{:S(2)}) async-start(bf16[4,44,288]{2,1,0:T(8,128)(2,1)} %all_to_all.28), calls=%async_computation | async-start | bytes 294912 | tf_op jit(solution)/shard_map/all_to_all | solution.py:42
  14.3 8.1 %all-gather = bf16[4,288,176]{1,2,0:T(8,128)(2,1)S(1)} all-gather(bf16[1,288,176]{1,2,0:T(8,128)(2,1)} %bitcast.39), channel_id=1, replica_groups=mesh['blk'=8,'feat'=4] {'feat'}, dimensions={0}, use_global_device_ids=true | all-gather | bytes 506880 | tf_op jit(solution)/shard_map/all_gather | solution.py:41
  22.4 0.2 copy.17
  22.6 0.4 reshape.11
  23.2 0.3 select_convert_fusion
  23.7 0.3 fusion.8
  24.0 78.5 %while.14 = (s32[]{:T(128)}, bf16[44,1152]{1,0:T(8,128)(2,1)S(1)}, f32[44,1152]{1,0:T(8,128)S(1)}, f32[176,1152]{1,0:T(8,128)S(1)}, f32[]{:T(128)}, /*index=5*/bf16[176,1152]{1,0:T(8,128)(2,1)S(1)}, f32[]{:T(128)}, s32[]{:T(128)}) while((s32[]{:T(128)}, bf16[44,1152]{1,0:T(8,128)(2,1)S(1)}, f32[44,1152]{1,0:T(8,128)S(1)}, ...), condition=%wide.region_1.2_spmd, body=%wide.region_0.1_spmd.sunk | while | flops 53826432 | bytes 4507181 | solution.py:53
  24.0 2.0 %collective-permute-start = (bf16[44,1152]{1,0:T(8,128)(2,1)S(1)}, bf16[44,1152]{1,0:T(8,128)(2,1)S(1)}, u32[]{:S(2)}, u32[]{:S(2)}) collective-permute-start(bf16[44,1152]{1,0:T(8,128)(2,1)S(1)} %get-tuple-element.108), channel_id=1, source_target_pairs={{28,0},{0,4},{4,8},{8,12},{12,16},{16,20},{20,24},{24,28},{29,1},{... | collective-permute-start | bytes 304136 | tf_op jit(solution)/shard_map/while/body/eval_jaxpr/ppermute | solution.py:10
  26.0 1.5 %collective-permute-start.1 = (f32[44,1152]{1,0:T(8,128)S(1)}, f32[44,1152]{1,0:T(8,128)S(1)}, u32[]{:S(2)}, u32[]{:S(2)}) collective-permute-start(f32[44,1152]{1,0:T(8,128)S(1)} %get-tuple-element.109), channel_id=1, source_target_pairs={{28,0},{0,4},{4,8},{8,12},{12,16},{16,20},{20,24},{24,28},{29,1},{... | collective-permute-start | bytes 608264 | tf_op jit(solution)/shard_map/while/body/eval_jaxpr/ppermute | solution.py:10
  27.6 5.4 %collective-permute-done = bf16[44,1152]{1,0:T(8,128)(2,1)S(1)} collective-permute-done((bf16[44,1152]{1,0:T(8,128)(2,1)S(1)}, bf16[44,1152]{1,0:T(8,128)(2,1)S(1)}, u32[]{:S(2)}, u32[]{:S(2)}) %collective-permute-start) | collective-permute-done | bytes 101408 | tf_op jit(solution)/shard_map/while/body/eval_jaxpr/ppermute | solution.py:10
  33.0 1.6 %fusion.34 = bf16[176,44]{0,1:T(8,128)(2,1)S(1)} fusion(bf16[176,1152]{1,0:T(8,128)(2,1)S(1)} %get-tuple-element.120, bf16[44,1152]{1,0:T(8,128)(2,1)S(1)} %collective-permute-done, f32[]{:T(128)} %get-tuple-element.121, f32[]{:T(128)} %get-tuple-element.119), kind=kOutput, calls=%fused_computation.8.clone.1 | convolution fusion | flops 17888640 | bytes 522376 | tf_op jit(solution)/shard_map/while/body/eval_jaxpr/dot_general | solution.py:14
  34.6 0.3 convolution_add_fusion.5
  34.9 2.5 %collective-permute-done.1 = f32[44,1152]{1,0:T(8,128)S(1)} collective-permute-done((f32[44,1152]{1,0:T(8,128)S(1)}, f32[44,1152]{1,0:T(8,128)S(1)}, u32[]{:S(2)}, u32[]{:S(2)}) %collective-permute-start.1) | collective-permute-done | bytes 202784 | tf_op jit(solution)/shard_map/while/body/eval_jaxpr/ppermute | solution.py:10
  37.4 0.2 convolution_add_fusion.4
  37.7 1.1 collective-permute-start.1
  38.8 7.5 %collective-permute-done = bf16[44,1152]{1,0:T(8,128)(2,1)S(1)} collective-permute-done((bf16[44,1152]{1,0:T(8,128)(2,1)S(1)}, bf16[44,1152]{1,0:T(8,128)(2,1)S(1)}, u32[]{:S(2)}, u32[]{:S(2)}) %collective-permute-start) | collective-permute-done | bytes 101408 | tf_op jit(solution)/shard_map/while/body/eval_jaxpr/ppermute | solution.py:10
  46.3 1.6 %fusion.34 = bf16[176,44]{0,1:T(8,128)(2,1)S(1)} fusion(bf16[176,1152]{1,0:T(8,128)(2,1)S(1)} %get-tuple-element.120, bf16[44,1152]{1,0:T(8,128)(2,1)S(1)} %collective-permute-done, f32[]{:T(128)} %get-tuple-element.121, f32[]{:T(128)} %get-tuple-element.119), kind=kOutput, calls=%fused_computation.8.clone.1 | convolution fusion | flops 17888640 | bytes 522376 | tf_op jit(solution)/shard_map/while/body/eval_jaxpr/dot_general | solution.py:14
  47.9 0.3 convolution_add_fusion.5
  48.2 1.6 %collective-permute-done.1 = f32[44,1152]{1,0:T(8,128)S(1)} collective-permute-done((f32[44,1152]{1,0:T(8,128)S(1)}, f32[44,1152]{1,0:T(8,128)S(1)}, u32[]{:S(2)}, u32[]{:S(2)}) %collective-permute-start.1) | collective-permute-done | bytes 202784 | tf_op jit(solution)/shard_map/while/body/eval_jaxpr/ppermute | solution.py:10
  50.2 8.6 %collective-permute-done = bf16[44,1152]{1,0:T(8,128)(2,1)S(1)} collective-permute-done((bf16[44,1152]{1,0:T(8,128)(2,1)S(1)}, bf16[44,1152]{1,0:T(8,128)(2,1)S(1)}, u32[]{:S(2)}, u32[]{:S(2)}) %collective-permute-start) | collective-permute-done | bytes 101408 | tf_op jit(solution)/shard_map/while/body/eval_jaxpr/ppermute | solution.py:10
  58.8 1.6 %fusion.34 = bf16[176,44]{0,1:T(8,128)(2,1)S(1)} fusion(bf16[176,1152]{1,0:T(8,128)(2,1)S(1)} %get-tuple-element.120, bf16[44,1152]{1,0:T(8,128)(2,1)S(1)} %collective-permute-done, f32[]{:T(128)} %get-tuple-element.121, f32[]{:T(128)} %get-tuple-element.119), kind=kOutput, calls=%fused_computation.8.clone.1 | convolution fusion | flops 17888640 | bytes 522376 | tf_op jit(solution)/shard_map/while/body/eval_jaxpr/dot_general | solution.py:14
  60.4 0.3 convolution_add_fusion.5
  60.7 0.7 collective-permute-done.1
  61.7 7.9 %collective-permute-done = bf16[44,1152]{1,0:T(8,128)(2,1)S(1)} collective-permute-done((bf16[44,1152]{1,0:T(8,128)(2,1)S(1)}, bf16[44,1152]{1,0:T(8,128)(2,1)S(1)}, u32[]{:S(2)}, u32[]{:S(2)}) %collective-permute-start) | collective-permute-done | bytes 101408 | tf_op jit(solution)/shard_map/while/body/eval_jaxpr/ppermute | solution.py:10
  69.7 1.6 %fusion.34 = bf16[176,44]{0,1:T(8,128)(2,1)S(1)} fusion(bf16[176,1152]{1,0:T(8,128)(2,1)S(1)} %get-tuple-element.120, bf16[44,1152]{1,0:T(8,128)(2,1)S(1)} %collective-permute-done, f32[]{:T(128)} %get-tuple-element.121, f32[]{:T(128)} %get-tuple-element.119), kind=kOutput, calls=%fused_computation.8.clone.1 | convolution fusion | flops 17888640 | bytes 522376 | tf_op jit(solution)/shard_map/while/body/eval_jaxpr/dot_general | solution.py:14
  71.3 0.3 convolution_add_fusion.5
  71.6 0.4 collective-permute-done.1
  72.4 7.4 %collective-permute-done = bf16[44,1152]{1,0:T(8,128)(2,1)S(1)} collective-permute-done((bf16[44,1152]{1,0:T(8,128)(2,1)S(1)}, bf16[44,1152]{1,0:T(8,128)(2,1)S(1)}, u32[]{:S(2)}, u32[]{:S(2)}) %collective-permute-start) | collective-permute-done | bytes 101408 | tf_op jit(solution)/shard_map/while/body/eval_jaxpr/ppermute | solution.py:10
  79.7 1.6 %fusion.34 = bf16[176,44]{0,1:T(8,128)(2,1)S(1)} fusion(bf16[176,1152]{1,0:T(8,128)(2,1)S(1)} %get-tuple-element.120, bf16[44,1152]{1,0:T(8,128)(2,1)S(1)} %collective-permute-done, f32[]{:T(128)} %get-tuple-element.121, f32[]{:T(128)} %get-tuple-element.119), kind=kOutput, calls=%fused_computation.8.clone.1 | convolution fusion | flops 17888640 | bytes 522376 | tf_op jit(solution)/shard_map/while/body/eval_jaxpr/dot_general | solution.py:14
  81.3 0.3 convolution_add_fusion.5
  81.7 0.4 collective-permute-done.1
  82.4 7.4 %collective-permute-done = bf16[44,1152]{1,0:T(8,128)(2,1)S(1)} collective-permute-done((bf16[44,1152]{1,0:T(8,128)(2,1)S(1)}, bf16[44,1152]{1,0:T(8,128)(2,1)S(1)}, u32[]{:S(2)}, u32[]{:S(2)}) %collective-permute-start) | collective-permute-done | bytes 101408 | tf_op jit(solution)/shard_map/while/body/eval_jaxpr/ppermute | solution.py:10
  89.8 1.6 %fusion.34 = bf16[176,44]{0,1:T(8,128)(2,1)S(1)} fusion(bf16[176,1152]{1,0:T(8,128)(2,1)S(1)} %get-tuple-element.120, bf16[44,1152]{1,0:T(8,128)(2,1)S(1)} %collective-permute-done, f32[]{:T(128)} %get-tuple-element.121, f32[]{:T(128)} %get-tuple-element.119), kind=kOutput, calls=%fused_computation.8.clone.1 | convolution fusion | flops 17888640 | bytes 522376 | tf_op jit(solution)/shard_map/while/body/eval_jaxpr/dot_general | solution.py:14
  91.4 0.3 convolution_add_fusion.5
  91.7 0.4 collective-permute-done.1
  92.2 0.2 convolution_add_fusion.4
  92.5 7.4 %collective-permute-done = bf16[44,1152]{1,0:T(8,128)(2,1)S(1)} collective-permute-done((bf16[44,1152]{1,0:T(8,128)(2,1)S(1)}, bf16[44,1152]{1,0:T(8,128)(2,1)S(1)}, u32[]{:S(2)}, u32[]{:S(2)}) %collective-permute-start) | collective-permute-done | bytes 101408 | tf_op jit(solution)/shard_map/while/body/eval_jaxpr/ppermute | solution.py:10
  99.9 1.6 %fusion.34 = bf16[176,44]{0,1:T(8,128)(2,1)S(1)} fusion(bf16[176,1152]{1,0:T(8,128)(2,1)S(1)} %get-tuple-element.120, bf16[44,1152]{1,0:T(8,128)(2,1)S(1)} %collective-permute-done, f32[]{:T(128)} %get-tuple-element.121, f32[]{:T(128)} %get-tuple-element.119), kind=kOutput, calls=%fused_computation.8.clone.1 | convolution fusion | flops 17888640 | bytes 522376 | tf_op jit(solution)/shard_map/while/body/eval_jaxpr/dot_general | solution.py:14
  101.5 0.3 convolution_add_fusion.5
  101.8 0.4 collective-permute-done.1
  102.5 1.4 %copy.19 = f32[176,1152]{0,1:T(8,128)} copy(f32[176,1152]{1,0:T(8,128)S(1)} %get-tuple-element.40) | data formatting | bytes 1622016
  104.0 8.6 %collective-permute-done.2 = f32[44,1152]{1,0:T(8,128)S(1)} collective-permute-done((f32[44,1152]{1,0:T(8,128)S(1)}, f32[44,1152]{1,0:T(8,128)S(1)}, u32[]{:S(2)}, u32[]{:S(2)}) %collective-permute-start.2) | collective-permute-done | bytes 202784 | tf_op jit(solution)/shard_map/ppermute | solution.py:10
  112.8 8.9 %all_to_all.38 = f32[44,4,288]{2,0,1:T(8,128)S(1)} all-to-all(f32[44,4,288]{2,0,1:T(8,128)S(1)} %copy.18), channel_id=1, replica_groups=mesh['blk'=8,'feat'=4] {'feat'}, dimensions={1} | all-to-all | bytes 405504 | tf_op jit(solution)/shard_map/all_to_all | solution.py:58
  121.7 0.7 all_to_all.35
  122.4 7.1 %reduce-scatter.4.cloned.1.call-done = f32[288,176]{1,0:T(8,128)} async-done(((f32[1152,176]{1,0:T(8,128)}), f32[288,176]{1,0:T(8,128)}) %reduce-scatter.4.cloned.1.call-update) | async-done | bytes 202768
  129.6 1.1 copy.20
  130.7 0.7 broadcast_multiply_fusion
  (34 shorter events, 2.5 us)
Async XLA Ops:
  8.8 14.2 %all-to-all-start = ((bf16[4,44,288]{2,1,0:T(8,128)(2,1)}), bf16[4,44,288]{2,1,0:T(8,128)(2,1)S(1)}, u32[]{:S(2)}, u32[]{:S(2)}) async-start(bf16[4,44,288]{2,1,0:T(8,128)(2,1)} %all_to_all.28), calls=%async_computation | async-start | bytes 294912 | tf_op jit(solution)/shard_map/all_to_all | solution.py:42
  13.0 116.6 %reduce-scatter.4.cloned.1.call-start = ((), (), s32[]{:S(2)}) async-start(), calls=%async_computation.3 | async-start | bytes 1474560
  24.0 9.0 %collective-permute-start = (bf16[44,1152]{1,0:T(8,128)(2,1)S(1)}, bf16[44,1152]{1,0:T(8,128)(2,1)S(1)}, u32[]{:S(2)}, u32[]{:S(2)}) collective-permute-start(bf16[44,1152]{1,0:T(8,128)(2,1)S(1)} %get-tuple-element.108), channel_id=1, source_target_pairs={{28,0},{0,4},{4,8},{8,12},{12,16},{16,20},{20,24},{24,28},{29,1},{... | collective-permute-start | bytes 304136 | tf_op jit(solution)/shard_map/while/body/eval_jaxpr/ppermute | solution.py:10
  26.0 11.4 %collective-permute-start.1 = (f32[44,1152]{1,0:T(8,128)S(1)}, f32[44,1152]{1,0:T(8,128)S(1)}, u32[]{:S(2)}, u32[]{:S(2)}) collective-permute-start(f32[44,1152]{1,0:T(8,128)S(1)} %get-tuple-element.109), channel_id=1, source_target_pairs={{28,0},{0,4},{4,8},{8,12},{12,16},{16,20},{20,24},{24,28},{29,1},{... | collective-permute-start | bytes 608264 | tf_op jit(solution)/shard_map/while/body/eval_jaxpr/ppermute | solution.py:10
  37.6 8.7 %collective-permute-start = (bf16[44,1152]{1,0:T(8,128)(2,1)S(1)}, bf16[44,1152]{1,0:T(8,128)(2,1)S(1)}, u32[]{:S(2)}, u32[]{:S(2)}) collective-permute-start(bf16[44,1152]{1,0:T(8,128)(2,1)S(1)} %get-tuple-element.108), channel_id=1, source_target_pairs={{28,0},{0,4},{4,8},{8,12},{12,16},{16,20},{20,24},{24,28},{29,1},{... | collective-permute-start | bytes 304136 | tf_op jit(solution)/shard_map/while/body/eval_jaxpr/ppermute | solution.py:10
  37.7 12.2 %collective-permute-start.1 = (f32[44,1152]{1,0:T(8,128)S(1)}, f32[44,1152]{1,0:T(8,128)S(1)}, u32[]{:S(2)}, u32[]{:S(2)}) collective-permute-start(f32[44,1152]{1,0:T(8,128)S(1)} %get-tuple-element.109), channel_id=1, source_target_pairs={{28,0},{0,4},{4,8},{8,12},{12,16},{16,20},{20,24},{24,28},{29,1},{... | collective-permute-start | bytes 608264 | tf_op jit(solution)/shard_map/while/body/eval_jaxpr/ppermute | solution.py:10
  50.0 8.7 %collective-permute-start = (bf16[44,1152]{1,0:T(8,128)(2,1)S(1)}, bf16[44,1152]{1,0:T(8,128)(2,1)S(1)}, u32[]{:S(2)}, u32[]{:S(2)}) collective-permute-start(bf16[44,1152]{1,0:T(8,128)(2,1)S(1)} %get-tuple-element.108), channel_id=1, source_target_pairs={{28,0},{0,4},{4,8},{8,12},{12,16},{16,20},{20,24},{24,28},{29,1},{... | collective-permute-start | bytes 304136 | tf_op jit(solution)/shard_map/while/body/eval_jaxpr/ppermute | solution.py:10
  50.1 11.3 %collective-permute-start.1 = (f32[44,1152]{1,0:T(8,128)S(1)}, f32[44,1152]{1,0:T(8,128)S(1)}, u32[]{:S(2)}, u32[]{:S(2)}) collective-permute-start(f32[44,1152]{1,0:T(8,128)S(1)} %get-tuple-element.109), channel_id=1, source_target_pairs={{28,0},{0,4},{4,8},{8,12},{12,16},{16,20},{20,24},{24,28},{29,1},{... | collective-permute-start | bytes 608264 | tf_op jit(solution)/shard_map/while/body/eval_jaxpr/ppermute | solution.py:10
  61.6 8.1 %collective-permute-start = (bf16[44,1152]{1,0:T(8,128)(2,1)S(1)}, bf16[44,1152]{1,0:T(8,128)(2,1)S(1)}, u32[]{:S(2)}, u32[]{:S(2)}) collective-permute-start(bf16[44,1152]{1,0:T(8,128)(2,1)S(1)} %get-tuple-element.108), channel_id=1, source_target_pairs={{28,0},{0,4},{4,8},{8,12},{12,16},{16,20},{20,24},{24,28},{29,1},{... | collective-permute-start | bytes 304136 | tf_op jit(solution)/shard_map/while/body/eval_jaxpr/ppermute | solution.py:10
  61.7 10.4 %collective-permute-start.1 = (f32[44,1152]{1,0:T(8,128)S(1)}, f32[44,1152]{1,0:T(8,128)S(1)}, u32[]{:S(2)}, u32[]{:S(2)}) collective-permute-start(f32[44,1152]{1,0:T(8,128)S(1)} %get-tuple-element.109), channel_id=1, source_target_pairs={{28,0},{0,4},{4,8},{8,12},{12,16},{16,20},{20,24},{24,28},{29,1},{... | collective-permute-start | bytes 608264 | tf_op jit(solution)/shard_map/while/body/eval_jaxpr/ppermute | solution.py:10
  72.2 7.5 %collective-permute-start = (bf16[44,1152]{1,0:T(8,128)(2,1)S(1)}, bf16[44,1152]{1,0:T(8,128)(2,1)S(1)}, u32[]{:S(2)}, u32[]{:S(2)}) collective-permute-start(bf16[44,1152]{1,0:T(8,128)(2,1)S(1)} %get-tuple-element.108), channel_id=1, source_target_pairs={{28,0},{0,4},{4,8},{8,12},{12,16},{16,20},{20,24},{24,28},{29,1},{... | collective-permute-start | bytes 304136 | tf_op jit(solution)/shard_map/while/body/eval_jaxpr/ppermute | solution.py:10
  72.3 9.8 %collective-permute-start.1 = (f32[44,1152]{1,0:T(8,128)S(1)}, f32[44,1152]{1,0:T(8,128)S(1)}, u32[]{:S(2)}, u32[]{:S(2)}) collective-permute-start(f32[44,1152]{1,0:T(8,128)S(1)} %get-tuple-element.109), channel_id=1, source_target_pairs={{28,0},{0,4},{4,8},{8,12},{12,16},{16,20},{20,24},{24,28},{29,1},{... | collective-permute-start | bytes 608264 | tf_op jit(solution)/shard_map/while/body/eval_jaxpr/ppermute | solution.py:10
  82.3 7.5 %collective-permute-start = (bf16[44,1152]{1,0:T(8,128)(2,1)S(1)}, bf16[44,1152]{1,0:T(8,128)(2,1)S(1)}, u32[]{:S(2)}, u32[]{:S(2)}) collective-permute-start(bf16[44,1152]{1,0:T(8,128)(2,1)S(1)} %get-tuple-element.108), channel_id=1, source_target_pairs={{28,0},{0,4},{4,8},{8,12},{12,16},{16,20},{20,24},{24,28},{29,1},{... | collective-permute-start | bytes 304136 | tf_op jit(solution)/shard_map/while/body/eval_jaxpr/ppermute | solution.py:10
  82.4 9.8 %collective-permute-start.1 = (f32[44,1152]{1,0:T(8,128)S(1)}, f32[44,1152]{1,0:T(8,128)S(1)}, u32[]{:S(2)}, u32[]{:S(2)}) collective-permute-start(f32[44,1152]{1,0:T(8,128)S(1)} %get-tuple-element.109), channel_id=1, source_target_pairs={{28,0},{0,4},{4,8},{8,12},{12,16},{16,20},{20,24},{24,28},{29,1},{... | collective-permute-start | bytes 608264 | tf_op jit(solution)/shard_map/while/body/eval_jaxpr/ppermute | solution.py:10
  92.4 7.5 %collective-permute-start = (bf16[44,1152]{1,0:T(8,128)(2,1)S(1)}, bf16[44,1152]{1,0:T(8,128)(2,1)S(1)}, u32[]{:S(2)}, u32[]{:S(2)}) collective-permute-start(bf16[44,1152]{1,0:T(8,128)(2,1)S(1)} %get-tuple-element.108), channel_id=1, source_target_pairs={{28,0},{0,4},{4,8},{8,12},{12,16},{16,20},{20,24},{24,28},{29,1},{... | collective-permute-start | bytes 304136 | tf_op jit(solution)/shard_map/while/body/eval_jaxpr/ppermute | solution.py:10
  92.5 9.8 %collective-permute-start.1 = (f32[44,1152]{1,0:T(8,128)S(1)}, f32[44,1152]{1,0:T(8,128)S(1)}, u32[]{:S(2)}, u32[]{:S(2)}) collective-permute-start(f32[44,1152]{1,0:T(8,128)S(1)} %get-tuple-element.109), channel_id=1, source_target_pairs={{28,0},{0,4},{4,8},{8,12},{12,16},{16,20},{20,24},{24,28},{29,1},{... | collective-permute-start | bytes 608264 | tf_op jit(solution)/shard_map/while/body/eval_jaxpr/ppermute | solution.py:10
  103.9 8.7 %collective-permute-start.2 = (f32[44,1152]{1,0:T(8,128)S(1)}, f32[44,1152]{1,0:T(8,128)S(1)}, u32[]{:S(2)}, u32[]{:S(2)}) collective-permute-start(f32[44,1152]{1,0:T(8,128)S(1)} %get-tuple-element.41), channel_id=1, source_target_pairs={{28,0},{0,4},{4,8},{8,12},{12,16},{16,20},{20,24},{24,28},{29,1},{... | collective-permute-start | bytes 608264 | tf_op jit(solution)/shard_map/ppermute | solution.py:10
Sparse Core Ops, SparseCore 0:
  104.0 25.5 reduce-scatter.3
where the time goes:
time: 139 us; the launch traced here: 138 us
  waiting for transfers between devices  73.9 us (53%)
  blocking collectives  17 us (12%)
  matrix products  15.5 us (11%)
  between operations  15.4 us (11%)
  starting transfers between devices  9.57 us (7%)
  local copies, waits for them, and re-layouts  5.89 us (4%)
    ppermute x15, waiting for transfers between devices, from_behind(): return lax.ppermute(block, axis, route)  66.7 us
    dot_general x8, matrix products, pair_grads(): lax.dot_general(image_all, current, (((1,), (1,)), ((), ())), preferred_e...  11.4 us
    all_to_all x1, blocking collectives, shards(): lax.all_to_all(scale * text_acc, 'feat', split_axis=1, concat_axis=0, til...  8.87 us
    all_gather x1, blocking collectives, shards(): image_all = lax.all_gather(image, 'feat', axis=1, tiled=True)  8.09 us
    unnamed x2, waiting for transfers between devices  7.14 us
    ppermute x15, starting transfers between devices, from_behind(): return lax.ppermute(block, axis, route)  5.36 us
    all_to_all x1, starting transfers between devices, shards(): lax.all_to_all(text, 'feat', split_axis=0, concat_axis=1, tiled=True)  4.21 us
    unnamed x3, local copies, waits for them, and re-layouts  2.86 us
  transfers between devices with their start and end apart: 17, of which 16 were waited for; matrix products, arithmetic and copies ran while one was open for 10% of the time, Pallas kernels for 0%

commit v1 on v0

--- a/solution.py
+++ b/solution.py
@@ -1,6 +1,9 @@
+import functools
 import jax
 import jax.numpy as jnp
 from jax import lax
+from jax.experimental import pallas as pl
+from jax.experimental.pallas import tpu as pltpu
 from jax.sharding import PartitionSpec as P
 
 
@@ -59,7 +62,222 @@
     return (image_grad, text_grad)
 
 
+MESH = pl.DeviceIdType.MESH
+BF16 = jnp.bfloat16
+F32 = jnp.float32
+GROUP = 32
+
+
+def round_up(value, unit):
+    return -(-value // unit) * unit
+
+
+def dot_nt(a, b):
+    return lax.dot_general(a, b, (((1,), (1,)), ((), ())), preferred_element_type=F32)
+
+
+def kernel(nz, rows, wide, rem, img_ref, txt_ref, sc_ref, gi_ref, gt_ref,
+           buf, rbuf, acc, accr, ssem, rsem):
+    blk, feat = lax.axis_index("blk"), lax.axis_index("feat")
+    z, y = blk // 2, blk % 2
+    x, c = feat // 2, feat % 2
+    blk_y = z * 2 + 1 - y
+    feat_x = (1 - x) * 2 + c
+    feat_c = x * 2 + 1 - c
+    feat_xc = (1 - x) * 2 + 1 - c
+    near = jnp.minimum(z, nz - 1 - z)
+    has_up, has_down = z < nz - 1, z > 0
+
+    barrier = pltpu.get_barrier_semaphore()
+
+    def greet(b, f):
+        pl.semaphore_signal(barrier, inc=1, device_id=(b, f), device_id_type=MESH)
+
+    greet(blk_y, feat)
+    greet(blk, feat_x)
+    greet(blk, feat_c)
+
+    @pl.when(has_up)
+    def _():
+        greet(blk + 2, feat)
+
+    @pl.when(has_down)
+    def _():
+        greet(blk - 2, feat)
+
+    for t, ref in ((0, img_ref), (1, txt_ref)):
+        buf[t, blk, feat, 0:rows, :] = ref[:, 0:wide]
+        last = ref[:, wide:wide + rem]
+        for q in range(-(-rows // GROUP)):
+            n = min(GROUP, rows - q * GROUP)
+            buf[t, blk, feat, rows:rows + n, q * rem:(q + 1) * rem] = last[q * GROUP:q * GROUP + n]
+
+    pl.semaphore_wait(barrier, 3 + jnp.where(has_up, 1, 0) + jnp.where(has_down, 1, 0))
+
+    sent = []
+
+    def copy(t, b, f, to, sid):
+        return pltpu.make_async_remote_copy(
+            src_ref=buf.at[t, b, f], dst_ref=buf.at[t, b, f],
+            send_sem=ssem.at[sid], recv_sem=rsem.at[t, b, f],
+            device_id=to, device_id_type=MESH,
+        )
+
+    def send(t, b, f, to, cond=None):
+        sid = len(sent)
+        sent.append((t, b, f, to, cond))
+        if cond is None:
+            copy(t, b, f, to, sid).start()
+        else:
+            @pl.when(cond)
+            def _():
+                copy(t, b, f, to, sid).start()
+
+    def arrive(t, b, f):
+        copy(t, b, f, (blk, feat_c), 0).wait_recv()
+
+    def item(i):
+        k = jnp.where(i <= 2 * near, (i + 1) // 2, i - near)
+        below = jnp.where(i <= 2 * near, i % 2, jnp.where(z > near, 1, 0))
+        return jnp.where(below == 1, z - k, z + k), below
+
+    def stage1(i):
+        if i == 0:
+            zi = z
+            for t in (0, 1):
+                send(t, blk, feat, (blk + 2, feat), has_up)
+                send(t, blk, feat, (blk - 2, feat), has_down)
+        else:
+            zi, below = item(i)
+            onward_up = jnp.logical_and(below == 1, has_up)
+            onward_down = jnp.logical_and(below == 0, has_down)
+            for t in (0, 1):
+                b = zi * 2 + y
+                arrive(t, b, feat)
+                send(t, b, feat, (blk + 2, feat), onward_up)
+                send(t, b, feat, (blk - 2, feat), onward_down)
+        b = zi * 2 + y
+        for t in (0, 1):
+            send(t, b, feat, (blk, feat_x))
+            send(t, b, feat, (blk_y, feat))
+        for t in (0, 1):
+            send(t, b, feat, (blk, feat_c))
+
+    def place(i):
+        zi = item(i)[0] if i else z
+        return zi * 2 + y, zi * 2 + 1 - y
+
+    def stage2(i):
+        own, other = place(i)
+        arrive(0, other, feat)
+        send(0, other, feat, (blk, feat_x))
+        send(0, other, feat, (blk, feat_c))
+        arrive(1, own, feat_x)
+        send(1, own, feat_x, (blk_y, feat))
+        send(1, own, feat_x, (blk, feat_c))
+
+    def stage3(i):
+        own, other = place(i)
+        for t, b, f in ((0, own, feat_x), (1, other, feat), (0, other, feat_x), (1, other, feat_x)):
+            arrive(t, b, f)
+            send(t, b, f, (blk, feat_c))
+
+    scale, bias = sc_ref[0], sc_ref[1]
+
+    def unpack(b):
+        for t in (0, 1):
+            for q in range(-(-rows // GROUP)):
+                n = min(GROUP, rows - q * GROUP)
+                for f in range(4):
+                    rbuf[t, b, q * GROUP:q * GROUP + n, f * rem:(f + 1) * rem] = (
+                        buf[t, b, f, rows:rows + n, q * rem:(q + 1) * rem])
+
+    def work(b):
+        for t, u in ((0, 1), (1, 0)):
+            dots = dot_nt(rbuf[t, blk], rbuf[u, b])
+            for f in range(4):
+                dots += dot_nt(buf[t, blk, f, 0:rows, :], buf[u, b, f, 0:rows, :])
+            logit = scale * dots + bias
+            r = lax.broadcasted_iota(jnp.int32, logit.shape, 0)
+            col = lax.broadcasted_iota(jnp.int32, logit.shape, 1) + (b - blk) * rows
+            diag = r == col
+            value = jax.nn.sigmoid(jnp.where(diag, -logit, logit))
+            slope = jnp.where(diag, -value, value).astype(BF16)
+            acc[t] += jnp.dot(slope, buf[u, b, feat, 0:rows, :], preferred_element_type=F32)
+            accr[t] += jnp.dot(slope, rbuf[u, b], preferred_element_type=F32)
+
+    def stage4(i):
+        own, other = place(i)
+        for t in (0, 1):
+            for b in (own, other):
+                for f in (feat_c, feat_xc):
+                    arrive(t, b, f)
+        if i == 0:
+            acc[...] = jnp.zeros_like(acc)
+            accr[...] = jnp.zeros_like(accr)
+        unpack(own)
+        unpack(other)
+
+        @pl.loop(0, 2)
+        def _(s):
+            work(own - y + s)
+
+    for r in range(nz + 3):
+        for lag, stage in enumerate((stage1, stage2, stage3, stage4)):
+            if 0 <= r - lag < nz:
+                stage(r - lag)
+
+    for t, ref in ((0, gi_ref), (1, gt_ref)):
+        ref[:, 0:wide] = scale * acc[t]
+        for f in range(4):
+            @pl.when(feat == f)
+            def _():
+                ref[:, wide:wide + rem] = scale * accr[t, :, f * rem:(f + 1) * rem]
+
+    for sid, (t, b, f, to, cond) in enumerate(sent):
+        if cond is None:
+            copy(t, b, f, to, sid).wait_send()
+        else:
+            @pl.when(cond)
+            def _():
+                copy(t, b, f, to, sid).wait_send()
+
+
+def gathered(blocks, image, text, scale, bias):
+    rows, width = image.shape
+    wide = width // 128 * 128
+    rem = width - wide
+    nz = blocks // 2
+    out = jax.ShapeDtypeStruct((rows, width), F32)
+    return pl.pallas_call(
+        functools.partial(kernel, nz, rows, wide, rem),
+        out_shape=(out, out),
+        in_specs=[pl.BlockSpec(memory_space=pltpu.VMEM)] * 2
+        + [pl.BlockSpec(memory_space=pltpu.SMEM)],
+        out_specs=(pl.BlockSpec(memory_space=pltpu.VMEM),) * 2,
+        scratch_shapes=[
+            pltpu.VMEM((2, blocks, 4, rows + GROUP, wide), BF16),
+            pltpu.VMEM((2, blocks, rows, 4 * rem), BF16),
+            pltpu.VMEM((2, rows, wide), F32),
+            pltpu.VMEM((2, rows, 4 * rem), F32),
+            pltpu.SemaphoreType.DMA((26 * nz,)),
+            pltpu.SemaphoreType.DMA((2, blocks, 4)),
+        ],
+        compiler_params=pltpu.CompilerParams(
+            collective_id=0, has_side_effects=True, vmem_limit_bytes=48 * 2**20
+        ),
+    )(image, text, jnp.stack([scale, bias]))
+
+
 def solution(mesh):
     in_specs = (P("blk", "feat"), P("blk", "feat"), P(), P())
     out_specs = (P("blk", "feat"), P("blk", "feat"))
-    return jax.shard_map(shards, mesh=mesh, in_specs=in_specs, out_specs=out_specs, check_vma=False)
+    blocks, feats = mesh.shape["blk"], mesh.shape["feat"]
+
+    def body(image, text, scale, bias):
+        whole = 2 * blocks * feats * image.size * 2
+        if feats == 4 and blocks % 2 == 0 and whole <= 16 * 2**20:
+            return gathered(blocks, image, text, scale, bias)
+        return shards(image, text, scale, bias)
+
+    return jax.shard_map(body, mesh=mesh, in_specs=in_specs, out_specs=out_specs, check_vma=False)

time: 139 us -> 47.5 us (0.34)
  waiting for transfers between devices: 73.9 us -> 0 us
  Pallas kernels: 0 us -> 42.1 us
  blocking collectives: 17 us -> 0 us
  matrix products: 15.5 us -> 0 us
  between operations: 15.4 us -> 1.93 us
  starting transfers between devices: 9.57 us -> 0 us
  local copies, waits for them, and re-layouts: 5.89 us -> 3.22 us
    ppermute x15 -> x0, waiting for transfers between devices: 66.7 us -> none  [from_behind(): return lax.ppermute(block, axis, route)]
    pallas_call x0 -> x1, Pallas kernels: none -> 42.1 us  [gathered(): pl.pallas_call(functools.partial(kernel, nz, rows, wide, rem), out_shape=...]
    dot_general x24 -> x0, matrix products: 15.5 us -> none  [the longest x8 11.4 us: pair_grads(): lax.dot_general(image_all, current, (((1,), (1,)), ((), ())), preferred_e...]
    all_to_all x1 -> x0, blocking collectives: 8.87 us -> none  [shards(): lax.all_to_all(scale * text_acc, 'feat', split_axis=1, concat_axis=0, til...]
    all_gather x1 -> x0, blocking collectives: 8.09 us -> none  [shards(): image_all = lax.all_gather(image, 'feat', axis=1, tiled=True)]
    unnamed x2 -> x0, waiting for transfers between devices: 7.14 us -> none
    ppermute x15 -> x0, starting transfers between devices: 5.36 us -> none  [from_behind(): return lax.ppermute(block, axis, route)]
    all_to_all x1 -> x0, starting transfers between devices: 4.21 us -> none  [shards(): lax.all_to_all(text, 'feat', split_axis=0, concat_axis=1, tiled=True)]
  transfers between devices with their start and end apart: 17 -> 0, of which waited for: 16 -> 0; matrix products, arithmetic and copies ran while one was open for 10% -> 0% of each run, Pallas kernels for 0% -> 0%
where the time goes in v1:
time: 47.5 us; the launch traced here: 47.3 us
  Pallas kernels  42.1 us (89%)
  local copies, waits for them, and re-layouts  3.22 us (7%)
  between operations  1.93 us (4%)
    pallas_call x1, Pallas kernels, gathered(): pl.pallas_call(functools.partial(kernel, nz, rows, wide, rem), out_shape=...  42.1 us
    unnamed x6, local copies, waits for them, and re-layouts  3.22 us

profile of v1, /device:TPU:0, one launch (start us, length us, event | category | flops | bytes accessed | tf_op | source)
XLA Modules:
  0.0 47.3 jit_solution(10873455769048136684)
XLA Ops:
  1.9 0.1 pad_maximum_fusion.sc_ref
  2.0 0.0 copy-start
  2.0 0.9 %copy-done = bf16[176,288]{1,0:T(8,128)(2,1)S(1)} copy-done((bf16[176,288]{1,0:T(8,128)(2,1)S(1)}, bf16[176,288]{1,0:T(8,128)(2,1)}, u32[]{:S(2)}) %copy-start) | copy-done | bytes 101400
  2.9 0.0 copy-start.1
  2.9 0.9 %copy-done.1 = bf16[176,288]{1,0:T(8,128)(2,1)S(1)} copy-done((bf16[176,288]{1,0:T(8,128)(2,1)S(1)}, bf16[176,288]{1,0:T(8,128)(2,1)}, u32[]{:S(2)}) %copy-start.1) | copy-done | bytes 101400
  3.8 42.1 %shard_map.59 = (f32[176,288]{1,0:T(8,128)S(1)}, f32[176,288]{1,0:T(8,128)S(1)}) custom-call(bf16[176,288]{1,0:T(8,128)(2,1)S(1)} %copy-done, bf16[176,288]{1,0:T(8,128)(2,1)S(1)} %copy-done.1, f32[2]{0:T(128)S(1)} %pad_maximum_fusion.sc_ref), custom_call_target="tpu_custom_call" | custom-call | tf_op jit(solution)/shard_map/pallas_call | solution.py:252
  45.9 0.7 %copy.10 = f32[176,288]{1,0:T(8,128)} copy(f32[176,288]{1,0:T(8,128)S(1)} %get-tuple-element.4) | data formatting | bytes 405504
  46.6 0.7 %copy.11 = f32[176,288]{1,0:T(8,128)} copy(f32[176,288]{1,0:T(8,128)S(1)} %get-tuple-element.5) | data formatting | bytes 405504
Async XLA Ops:
  2.0 0.9 %copy-start = (bf16[176,288]{1,0:T(8,128)(2,1)S(1)}, bf16[176,288]{1,0:T(8,128)(2,1)}, u32[]{:S(2)}) copy-start(bf16[176,288]{1,0:T(8,128)(2,1)} %img_ref.1) | copy-start | bytes 304132
  2.9 0.9 %copy-start.1 = (bf16[176,288]{1,0:T(8,128)(2,1)S(1)}, bf16[176,288]{1,0:T(8,128)(2,1)}, u32[]{:S(2)}) copy-start(bf16[176,288]{1,0:T(8,128)(2,1)} %txt_ref.1) | copy-start | bytes 304132

commit v2 on v1

--- a/solution.py
+++ b/solution.py
@@ -76,8 +76,8 @@
     return lax.dot_general(a, b, (((1,), (1,)), ((), ())), preferred_element_type=F32)
 
 
-def kernel(nz, rows, wide, rem, img_ref, txt_ref, sc_ref, gi_ref, gt_ref,
-           buf, rbuf, acc, accr, ssem, rsem):
+def kernel(nz, rows, wide, rem, img_ref, txt_ref, scale_ref, bias_ref, gi_ref, gt_ref,
+           own_in, in_sem, buf, rbuf, acc, accr, ssem, rsem):
     blk, feat = lax.axis_index("blk"), lax.axis_index("feat")
     z, y = blk // 2, blk % 2
     x, c = feat // 2, feat % 2
@@ -85,6 +85,17 @@
     feat_x = (1 - x) * 2 + c
     feat_c = x * 2 + 1 - c
     feat_xc = (1 - x) * 2 + 1 - c
+    cut = (rows + GROUP) * 2 // 5 // 16 * 16
+    parts = (
+        (0, 0, cut, "zyx"),
+        (1, 0, cut, "zxy"),
+        (0, cut, rows + GROUP - cut, "yzx"),
+        (1, cut, rows + GROUP - cut, "xzy"),
+    )
+    loads = [pltpu.make_async_copy(ref, own_in.at[t], in_sem.at[t])
+             for t, ref in enumerate((img_ref, txt_ref))]
+    for load in loads:
+        load.start()
     near = jnp.minimum(z, nz - 1 - z)
     has_up, has_down = z < nz - 1, z > 0
 
@@ -105,9 +116,10 @@
     def _():
         greet(blk - 2, feat)
 
-    for t, ref in ((0, img_ref), (1, txt_ref)):
-        buf[t, blk, feat, 0:rows, :] = ref[:, 0:wide]
-        last = ref[:, wide:wide + rem]
+    for t in (0, 1):
+        loads[t].wait()
+        buf[t, blk, feat, 0:rows, :] = own_in[t, :, 0:wide]
+        last = own_in[t, :, wide:wide + rem]
         for q in range(-(-rows // GROUP)):
             n = min(GROUP, rows - q * GROUP)
             buf[t, blk, feat, rows:rows + n, q * rem:(q + 1) * rem] = last[q * GROUP:q * GROUP + n]
@@ -116,73 +128,57 @@
 
     sent = []
 
-    def copy(t, b, f, to, sid):
+    def copy(p, b, f, to, sid):
+        t, first, n, _ = parts[p]
+        slot = buf.at[t, b, f, pl.ds(first, n)]
         return pltpu.make_async_remote_copy(
-            src_ref=buf.at[t, b, f], dst_ref=buf.at[t, b, f],
-            send_sem=ssem.at[sid], recv_sem=rsem.at[t, b, f],
+            src_ref=slot, dst_ref=slot, send_sem=ssem.at[sid], recv_sem=rsem.at[p, b, f],
             device_id=to, device_id_type=MESH,
         )
 
-    def send(t, b, f, to, cond=None):
+    def send(p, b, f, to, cond=None):
         sid = len(sent)
-        sent.append((t, b, f, to, cond))
+        sent.append((p, b, f, to, cond))
         if cond is None:
-            copy(t, b, f, to, sid).start()
+            copy(p, b, f, to, sid).start()
         else:
             @pl.when(cond)
             def _():
-                copy(t, b, f, to, sid).start()
-
-    def arrive(t, b, f):
-        copy(t, b, f, (blk, feat_c), 0).wait_recv()
+                copy(p, b, f, to, sid).start()
+
+    def arrive(p, b, f):
+        copy(p, b, f, (blk, feat_c), 0).wait_recv()
 
     def item(i):
         k = jnp.where(i <= 2 * near, (i + 1) // 2, i - near)
         below = jnp.where(i <= 2 * near, i % 2, jnp.where(z > near, 1, 0))
         return jnp.where(below == 1, z - k, z + k), below
 
-    def stage1(i):
-        if i == 0:
-            zi = z
-            for t in (0, 1):
-                send(t, blk, feat, (blk + 2, feat), has_up)
-                send(t, blk, feat, (blk - 2, feat), has_down)
-        else:
-            zi, below = item(i)
-            onward_up = jnp.logical_and(below == 1, has_up)
-            onward_down = jnp.logical_and(below == 0, has_down)
-            for t in (0, 1):
-                b = zi * 2 + y
-                arrive(t, b, feat)
-                send(t, b, feat, (blk + 2, feat), onward_up)
-                send(t, b, feat, (blk - 2, feat), onward_down)
-        b = zi * 2 + y
-        for t in (0, 1):
-            send(t, b, feat, (blk, feat_x))
-            send(t, b, feat, (blk_y, feat))
-        for t in (0, 1):
-            send(t, b, feat, (blk, feat_c))
-
-    def place(i):
+    def place(i, dy):
         zi = item(i)[0] if i else z
-        return zi * 2 + y, zi * 2 + 1 - y
-
-    def stage2(i):
-        own, other = place(i)
-        arrive(0, other, feat)
-        send(0, other, feat, (blk, feat_x))
-        send(0, other, feat, (blk, feat_c))
-        arrive(1, own, feat_x)
-        send(1, own, feat_x, (blk_y, feat))
-        send(1, own, feat_x, (blk, feat_c))
-
-    def stage3(i):
-        own, other = place(i)
-        for t, b, f in ((0, own, feat_x), (1, other, feat), (0, other, feat_x), (1, other, feat_x)):
-            arrive(t, b, f)
-            send(t, b, f, (blk, feat_c))
-
-    scale, bias = sc_ref[0], sc_ref[1]
+        return zi * 2 + (1 - y if dy else y)
+
+    def relay(p, i, dy, dx):
+        order = parts[p][3]
+        far = {"z": i, "y": dy, "x": dx}
+        came = max([n for n, axis in enumerate(order) if far[axis]], default=-1)
+        b, f = place(i, dy), feat_x if dx else feat
+        if came >= 0:
+            arrive(p, b, f)
+        ahead = order[came + 1:]
+        if came >= 0 and order[came] == "z":
+            below = item(i)[1]
+            send(p, b, f, (blk + 2, feat), jnp.logical_and(below == 1, has_up))
+            send(p, b, f, (blk - 2, feat), jnp.logical_and(below == 0, has_down))
+        for axis in ahead:
+            if axis == "z":
+                send(p, b, f, (blk + 2, feat), has_up)
+                send(p, b, f, (blk - 2, feat), has_down)
+            else:
+                send(p, b, f, (blk, feat_x) if axis == "x" else (blk_y, feat))
+        send(p, b, f, (blk, feat_c))
+
+    scale, bias = scale_ref[0], bias_ref[0]
 
     def unpack(b):
         for t in (0, 1):
@@ -206,41 +202,41 @@
             acc[t] += jnp.dot(slope, buf[u, b, feat, 0:rows, :], preferred_element_type=F32)
             accr[t] += jnp.dot(slope, rbuf[u, b], preferred_element_type=F32)
 
-    def stage4(i):
-        own, other = place(i)
-        for t in (0, 1):
-            for b in (own, other):
-                for f in (feat_c, feat_xc):
-                    arrive(t, b, f)
-        if i == 0:
+    def finish(i, dy):
+        b = place(i, dy)
+        for p in range(len(parts)):
+            for f in (feat_c, feat_xc):
+                arrive(p, b, f)
+        if i == 0 and dy == 0:
             acc[...] = jnp.zeros_like(acc)
             accr[...] = jnp.zeros_like(accr)
-        unpack(own)
-        unpack(other)
-
-        @pl.loop(0, 2)
-        def _(s):
-            work(own - y + s)
-
-    for r in range(nz + 3):
-        for lag, stage in enumerate((stage1, stage2, stage3, stage4)):
-            if 0 <= r - lag < nz:
-                stage(r - lag)
+        unpack(b)
+        work(b)
+
+    events = []
+    for i in range(nz):
+        for dy in (0, 1):
+            for dx in (0, 1):
+                for p in range(len(parts)):
+                    events.append((i + dy + dx, len(events), relay, (p, i, dy, dx)))
+            events.append((i + dy + 3, len(events), finish, (i, dy)))
+    for _, _, run, args in sorted(events, key=lambda event: event[:2]):
+        run(*args)
 
     for t, ref in ((0, gi_ref), (1, gt_ref)):
-        ref[:, 0:wide] = scale * acc[t]
+        ref[:, 0:wide] = acc[t]
         for f in range(4):
             @pl.when(feat == f)
             def _():
-                ref[:, wide:wide + rem] = scale * accr[t, :, f * rem:(f + 1) * rem]
-
-    for sid, (t, b, f, to, cond) in enumerate(sent):
+                ref[:, wide:wide + rem] = accr[t, :, f * rem:(f + 1) * rem]
+
+    for sid, (p, b, f, to, cond) in enumerate(sent):
         if cond is None:
-            copy(t, b, f, to, sid).wait_send()
+            copy(p, b, f, to, sid).wait_send()
         else:
             @pl.when(cond)
             def _():
-                copy(t, b, f, to, sid).wait_send()
+                copy(p, b, f, to, sid).wait_send()
 
 
 def gathered(blocks, image, text, scale, bias):
@@ -249,24 +245,27 @@
     rem = width - wide
     nz = blocks // 2
     out = jax.ShapeDtypeStruct((rows, width), F32)
-    return pl.pallas_call(
+    image_sum, text_sum = pl.pallas_call(
         functools.partial(kernel, nz, rows, wide, rem),
         out_shape=(out, out),
-        in_specs=[pl.BlockSpec(memory_space=pltpu.VMEM)] * 2
-        + [pl.BlockSpec(memory_space=pltpu.SMEM)],
+        in_specs=[pl.BlockSpec(memory_space=pltpu.HBM)] * 2
+        + [pl.BlockSpec(memory_space=pltpu.SMEM)] * 2,
         out_specs=(pl.BlockSpec(memory_space=pltpu.VMEM),) * 2,
         scratch_shapes=[
+            pltpu.VMEM((2, rows, width), BF16),
+            pltpu.SemaphoreType.DMA((2,)),
             pltpu.VMEM((2, blocks, 4, rows + GROUP, wide), BF16),
             pltpu.VMEM((2, blocks, rows, 4 * rem), BF16),
             pltpu.VMEM((2, rows, wide), F32),
             pltpu.VMEM((2, rows, 4 * rem), F32),
-            pltpu.SemaphoreType.DMA((26 * nz,)),
-            pltpu.SemaphoreType.DMA((2, blocks, 4)),
+            pltpu.SemaphoreType.DMA((44 * nz,)),
+            pltpu.SemaphoreType.DMA((4, blocks, 4)),
         ],
         compiler_params=pltpu.CompilerParams(
-            collective_id=0, has_side_effects=True, vmem_limit_bytes=48 * 2**20
+            collective_id=0, has_side_effects=True, vmem_limit_bytes=121 * 2**19
         ),
-    )(image, text, jnp.stack([scale, bias]))
+    )(image, text, scale.reshape(1), bias.reshape(1))
+    return scale * image_sum, scale * text_sum
 
 
 def solution(mesh):

time: 47.5 us -> 47.2 us (level)
  local copies, waits for them, and re-layouts: 3.22 us -> 0 us
  other arithmetic: 0.08 us -> 1.87 us
  Pallas kernels: 42.1 us -> 43.2 us
    unnamed x6 -> x0, local copies, waits for them, and re-layouts: 3.22 us -> none
    mul x0 -> x1, other arithmetic: none -> 1.87 us  [gathered(): return (scale * image_sum, scale * text_sum)]
    pallas_call x1, Pallas kernels: 42.1 us -> 43.2 us  [gathered(): pl.pallas_call(functools.partial(kernel, nz, rows, wide, rem), out_shape=...]
where the time goes in v2:
time: 47.2 us; the launch traced here: 47 us
  Pallas kernels  43.2 us (92%)
  between operations  1.93 us (4%)
  other arithmetic  1.87 us (4%)
    pallas_call x1, Pallas kernels, gathered(): pl.pallas_call(functools.partial(kernel, nz, rows, wide, rem), out_shape=...  43.2 us
    mul x1, other arithmetic, gathered(): return (scale * image_sum, scale * text_sum)  1.87 us

profile of v2, /device:TPU:0, one launch (start us, length us, event | category | flops | bytes accessed | tf_op | source)
XLA Modules:
  0.0 47.0 jit_solution(14500465564932162428)
XLA Ops:
  1.9 43.2 %shard_map.59 = (f32[176,288]{1,0:T(8,128)}, f32[176,288]{1,0:T(8,128)}) custom-call(bf16[176,288]{1,0:T(8,128)(2,1)} %img_ref.1, bf16[176,288]{1,0:T(8,128)(2,1)} %txt_ref.1, f32[1]{0:T(128)} %bitcast.2.scale_ref, f32[1]{0:T(128)} %bitcast.3.bias_ref), custom_call_target="tpu_custom_call" | custom-call | tf_op jit(solution)/shard_map/pallas_call | solution.py:248
  45.2 1.9 %broadcast_multiply_fusion = (f32[176,288]{1,0:T(8,128)}, f32[176,288]{1,0:T(8,128)}) fusion(f32[176,288]{1,0:T(8,128)} %get-tuple-element.5, f32[]{:T(128)} %copy.6, f32[176,288]{1,0:T(8,128)} %get-tuple-element.4), kind=kLoop, calls=%fused_computation | loop fusion | flops 101376 | bytes 811012 | tf_op jit(solution)/shard_map/mul | solution.py:268

commit v3 on v0

--- a/solution.py
+++ b/solution.py
@@ -1,6 +1,9 @@
+import functools
 import jax
 import jax.numpy as jnp
 from jax import lax
+from jax.experimental import pallas as pl
+from jax.experimental.pallas import tpu as pltpu
 from jax.sharding import PartitionSpec as P
 
 
@@ -59,7 +62,234 @@
     return (image_grad, text_grad)
 
 
+MESH = pl.DeviceIdType.MESH
+BF16 = jnp.bfloat16
+F32 = jnp.float32
+GROUP = 32
+
+
+def round_up(value, unit):
+    return -(-value // unit) * unit
+
+
+def dot_nt(a, b):
+    return lax.dot_general(a, b, (((1,), (1,)), ((), ())), preferred_element_type=F32)
+
+
+def kernel(nz, rows, wide, rem, img_ref, txt_ref, scale_ref, bias_ref, gi_ref, gt_ref,
+           own_in, in_sem, buf, slope_buf, mine, theirs, own_rem, acc, accr,
+           ssem, rsem, slope_ssem, slope_rsem):
+    blk, feat = lax.axis_index("blk"), lax.axis_index("feat")
+    z, y = blk // 2, blk % 2
+    x, c = feat // 2, feat % 2
+    u = 1 - c
+    blk_y = z * 2 + 1 - y
+    feat_x = (1 - x) * 2 + c
+    feat_c = x * 2 + 1 - c
+    feat_xc = (1 - x) * 2 + 1 - c
+    near = jnp.minimum(z, nz - 1 - z)
+    groups = -(-rows // GROUP)
+    cut = (rows + GROUP) * 5 // 8 // 16 * 16
+    ranges = ((0, cut), (cut, rows + GROUP - cut))
+    orders = (("zyx", "zxy"), ("yzx", "xzy"))
+
+    def item(i):
+        k = jnp.where(i <= 2 * near, (i + 1) // 2, i - near)
+        below = jnp.where(i <= 2 * near, i % 2, jnp.where(z > near, 1, 0))
+        return jnp.where(below == 1, z - k, z + k)
+
+    planes = [z] + [item(i) for i in range(1, nz)]
+
+    def place(i, dy):
+        return planes[i] * 2 + (1 - y if dy else y)
+
+    loads = [pltpu.make_async_copy(ref, own_in.at[t], in_sem.at[t])
+             for t, ref in enumerate((img_ref, txt_ref))]
+    for load in loads:
+        load.start()
+
+    barrier = pltpu.get_barrier_semaphore()
+    for to in [(blk_y, feat), (blk, feat_x), (blk, feat_c)] + [
+            (place(i, 0), feat) for i in range(1, nz)]:
+        pl.semaphore_signal(barrier, inc=1, device_id=to, device_id_type=MESH)
+
+    for t in (0, 1):
+        loads[t].wait()
+        buf[t, blk, feat, 0:rows, :] = own_in[t, :, 0:wide]
+        last = own_in[t, :, wide:wide + rem]
+        for q in range(groups):
+            n = min(GROUP, rows - q * GROUP)
+            buf[t, blk, feat, rows:rows + n, q * rem:(q + 1) * rem] = last[q * GROUP:q * GROUP + n]
+
+    pl.semaphore_wait(barrier, 3 + nz - 1)
+
+    sent = []
+
+    def copy(h, t, b, f, to, sid):
+        slot = buf.at[t, b, f, pl.ds(*ranges[h])]
+        return pltpu.make_async_remote_copy(
+            src_ref=slot, dst_ref=slot, send_sem=ssem.at[sid], recv_sem=rsem.at[h, t, b, f],
+            device_id=to, device_id_type=MESH,
+        )
+
+    def send(h, t, b, f, to, cond=None):
+        sid = len(sent)
+        sent.append((h, t, b, f, to, cond))
+        if cond is None:
+            copy(h, t, b, f, to, sid).start()
+        else:
+            @pl.when(cond)
+            def _():
+                copy(h, t, b, f, to, sid).start()
+
+    def wait_sent():
+        for sid, (h, t, b, f, to, cond) in enumerate(sent):
+            if cond is None:
+                copy(h, t, b, f, to, sid).wait_send()
+            else:
+                @pl.when(cond)
+                def _():
+                    copy(h, t, b, f, to, sid).wait_send()
+
+    def arrive(h, t, b, f):
+        copy(h, t, b, f, (blk, feat_c), 0).wait_recv()
+
+    def relay(h, t, i, dy, dx):
+        order = orders[h][t]
+        far = {"z": i, "y": dy, "x": dx}
+        came = max([n for n, axis in enumerate(order) if far[axis]], default=-1)
+        b, f = place(i, dy), feat_x if dx else feat
+        if came >= 0:
+            arrive(h, t, b, f)
+        for axis in order[came + 1:]:
+            if axis == "z":
+                for other in range(1, nz):
+                    send(h, t, b, f, (planes[other] * 2 + y, feat))
+            else:
+                send(h, t, b, f, (blk, feat_x) if axis == "x" else (blk_y, feat))
+        send(h, t, b, f, (blk, feat_c), None if i == 0 and dy == 0 else c == t)
+
+    scale, bias = scale_ref[0], bias_ref[0]
+
+    def unpack(out, t, b):
+        for q in range(groups):
+            n = min(GROUP, rows - q * GROUP)
+            for f in range(4):
+                out[q * GROUP:q * GROUP + n, f * rem:(f + 1) * rem] = (
+                    buf[t, b, f, rows:rows + n, q * rem:(q + 1) * rem])
+
+    def hand(b):
+        return pltpu.make_async_remote_copy(
+            src_ref=slope_buf.at[c, b], dst_ref=slope_buf.at[c, b],
+            send_sem=slope_ssem.at[b], recv_sem=slope_rsem.at[b],
+            device_id=(blk, feat_c), device_id_type=MESH,
+        )
+
+    def finish(i, dy):
+        b = place(i, dy)
+        for h in (0, 1):
+            for f in (feat_c, feat_xc):
+                arrive(h, u, b, f)
+                if i == 0 and dy == 0:
+                    arrive(h, c, b, f)
+        if i == 0 and dy == 0:
+            unpack(mine, c, b)
+            acc[...] = jnp.zeros_like(acc)
+            accr[...] = jnp.zeros_like(accr)
+        unpack(theirs, u, b)
+        dots = dot_nt(mine[...], theirs[...])
+        for f in range(4):
+            dots += dot_nt(buf[c, blk, f, 0:rows, :], buf[u, b, f, 0:rows, :])
+        logit = scale * dots + bias
+        if i == 0 and dy == 0:
+            diag = (lax.broadcasted_iota(jnp.int32, logit.shape, 0)
+                    == lax.broadcasted_iota(jnp.int32, logit.shape, 1))
+            value = jax.nn.sigmoid(jnp.where(diag, -logit, logit))
+            value = jnp.where(diag, -value, value)
+        else:
+            value = jax.nn.sigmoid(logit)
+        slope_buf[c, b] = value.astype(BF16)
+        hand(b).start()
+
+    def apply(i, dy):
+        b = place(i, dy)
+        for t in (0, 1):
+            for q in range(groups):
+                n = min(GROUP, rows - q * GROUP)
+                own_rem[t, q * GROUP:q * GROUP + n, :] = (
+                    buf[t, b, feat, rows:rows + n, q * rem:(q + 1) * rem])
+        pltpu.make_async_remote_copy(
+            src_ref=slope_buf.at[u, b], dst_ref=slope_buf.at[u, b],
+            send_sem=slope_ssem.at[b], recv_sem=slope_rsem.at[b],
+            device_id=(blk, feat_c), device_id_type=MESH,
+        ).wait_recv()
+        for t in (0, 1):
+            slope = slope_buf[t, b]
+            acc[t] += jnp.dot(slope, buf[1 - t, b, feat, 0:rows, :], preferred_element_type=F32)
+            accr[t] += jnp.dot(slope, own_rem[1 - t], preferred_element_type=F32)
+
+    events = []
+    for i in range(nz):
+        for dy in (0, 1):
+            for dx in (0, 1):
+                for h in (0, 1):
+                    for t in (0, 1):
+                        events.append((i + dy + dx, len(events), relay, (h, t, i, dy, dx)))
+            events.append((i + dy + 2.5, len(events), finish, (i, dy)))
+            events.append((i + dy + 3.6, len(events), apply, (i, dy)))
+    events.append((nz + 2.4, len(events), wait_sent, ()))
+    for _, _, run, args in sorted(events, key=lambda event: event[:2]):
+        run(*args)
+
+    for t, ref in ((0, gi_ref), (1, gt_ref)):
+        ref[:, 0:wide] = scale * acc[t]
+        ref[:, wide:wide + rem] = scale * accr[t]
+    for b in range(nz * 2):
+        hand(b).wait_send()
+
+
+def gathered(blocks, image, text, scale, bias):
+    rows, width = image.shape
+    wide = width // 128 * 128
+    rem = width - wide
+    nz = blocks // 2
+    out = jax.ShapeDtypeStruct((rows, width), F32)
+    return pl.pallas_call(
+        functools.partial(kernel, nz, rows, wide, rem),
+        out_shape=(out, out),
+        in_specs=[pl.BlockSpec(memory_space=pl.ANY)] * 2
+        + [pl.BlockSpec(memory_space=pltpu.SMEM)] * 2,
+        out_specs=(pl.BlockSpec(memory_space=pltpu.VMEM),) * 2,
+        scratch_shapes=[
+            pltpu.VMEM((2, rows, width), BF16),
+            pltpu.SemaphoreType.DMA((2,)),
+            pltpu.VMEM((2, blocks, 4, rows + GROUP, wide), BF16),
+            pltpu.VMEM((2, blocks, rows, rows), BF16),
+            pltpu.VMEM((rows, 4 * rem), BF16),
+            pltpu.VMEM((rows, 4 * rem), BF16),
+            pltpu.VMEM((2, rows, rem), BF16),
+            pltpu.VMEM((2, rows, wide), F32),
+            pltpu.VMEM((2, rows, rem), F32),
+            pltpu.SemaphoreType.DMA((44 * nz,)),
+            pltpu.SemaphoreType.DMA((2, 2, blocks, 4)),
+            pltpu.SemaphoreType.DMA((blocks,)),
+            pltpu.SemaphoreType.DMA((blocks,)),
+        ],
+        compiler_params=pltpu.CompilerParams(
+            collective_id=0, has_side_effects=True, vmem_limit_bytes=48 * 2**20
+        ),
+    )(image, text, scale.reshape(1), bias.reshape(1))
+
+
 def solution(mesh):
     in_specs = (P("blk", "feat"), P("blk", "feat"), P(), P())
     out_specs = (P("blk", "feat"), P("blk", "feat"))
-    return jax.shard_map(shards, mesh=mesh, in_specs=in_specs, out_specs=out_specs, check_vma=False)
+    blocks, feats = mesh.shape["blk"], mesh.shape["feat"]
+
+    def body(image, text, scale, bias):
+        whole = 2 * blocks * feats * image.size * 2
+        if feats == 4 and blocks % 2 == 0 and whole <= 16 * 2**20:
+            return gathered(blocks, image, text, scale, bias)
+        return shards(image, text, scale, bias)
+
+    return jax.shard_map(body, mesh=mesh, in_specs=in_specs, out_specs=out_specs, check_vma=False)

time: 139 us -> 56.9 us (0.41)
  the two profiles are of different devices: /device:TPU:0 before, /device:TPU:21 now
where the time goes in v3:
time: 56.9 us; the launch traced here: 56.7 us
  Pallas kernels  51.6 us (91%)
  local copies, waits for them, and re-layouts  3.22 us (6%)
  between operations  1.94 us (3%)
    pallas_call x1, Pallas kernels, gathered(): pl.pallas_call(functools.partial(kernel, nz, rows, wide, rem), out_shape=...  51.6 us
    unnamed x6, local copies, waits for them, and re-layouts  3.22 us

profile of v3, /device:TPU:21, one launch (start us, length us, event | category | flops | bytes accessed | tf_op | source)
XLA Modules:
  0.0 56.7 jit_solution(17116993374020864802)
XLA Ops:
  1.9 0.0 copy-start
  1.9 0.9 %copy-done = bf16[176,288]{1,0:T(8,128)(2,1)S(1)} copy-done((bf16[176,288]{1,0:T(8,128)(2,1)S(1)}, bf16[176,288]{1,0:T(8,128)(2,1)}, u32[]{:S(2)}) %copy-start) | copy-done | bytes 101400
  2.8 0.0 copy-start.1
  2.8 0.9 %copy-done.1 = bf16[176,288]{1,0:T(8,128)(2,1)S(1)} copy-done((bf16[176,288]{1,0:T(8,128)(2,1)S(1)}, bf16[176,288]{1,0:T(8,128)(2,1)}, u32[]{:S(2)}) %copy-start.1) | copy-done | bytes 101400
  3.7 51.6 %shard_map.59 = (f32[176,288]{1,0:T(8,128)S(1)}, f32[176,288]{1,0:T(8,128)S(1)}) custom-call(bf16[176,288]{1,0:T(8,128)(2,1)S(1)} %copy-done, bf16[176,288]{1,0:T(8,128)(2,1)S(1)} %copy-done.1, f32[1]{0:T(128)} %bitcast.2.scale_ref, f32[1]{0:T(128)} %bitcast.3.bias_ref), custom_call_target="tpu_custom_call" | custom-call | tf_op jit(solution)/shard_map/pallas_call | solution.py:257
  55.3 0.7 %copy.10 = f32[176,288]{1,0:T(8,128)} copy(f32[176,288]{1,0:T(8,128)S(1)} %get-tuple-element.4) | data formatting | bytes 405504
  56.0 0.7 %copy.11 = f32[176,288]{1,0:T(8,128)} copy(f32[176,288]{1,0:T(8,128)S(1)} %get-tuple-element.5) | data formatting | bytes 405504
Async XLA Ops:
  1.9 0.9 %copy-start = (bf16[176,288]{1,0:T(8,128)(2,1)S(1)}, bf16[176,288]{1,0:T(8,128)(2,1)}, u32[]{:S(2)}) copy-start(bf16[176,288]{1,0:T(8,128)(2,1)} %img_ref.1) | copy-start | bytes 304132
  2.8 0.9 %copy-start.1 = (bf16[176,288]{1,0:T(8,128)(2,1)S(1)}, bf16[176,288]{1,0:T(8,128)(2,1)}, u32[]{:S(2)}) copy-start(bf16[176,288]{1,0:T(8,128)(2,1)} %txt_ref.1) | copy-start | bytes 304132

commit v4 on v3

--- a/solution.py
+++ b/solution.py
@@ -89,7 +89,8 @@
     feat_xc = (1 - x) * 2 + 1 - c
     near = jnp.minimum(z, nz - 1 - z)
     groups = -(-rows // GROUP)
-    cut = (rows + GROUP) * 5 // 8 // 16 * 16
+    cut = (rows + GROUP) * 2 // 5 // 16 * 16
+    has_up, has_down = z < nz - 1, z > 0
     ranges = ((0, cut), (cut, rows + GROUP - cut))
     orders = (("zyx", "zxy"), ("yzx", "xzy"))
 
@@ -100,6 +101,15 @@
 
     planes = [z] + [item(i) for i in range(1, nz)]
 
+    def along_z(act):
+        @pl.when(has_up)
+        def _():
+            act((blk + 2, feat))
+
+        @pl.when(has_down)
+        def _():
+            act((blk - 2, feat))
+
     def place(i, dy):
         return planes[i] * 2 + (1 - y if dy else y)
 
@@ -109,9 +119,13 @@
         load.start()
 
     barrier = pltpu.get_barrier_semaphore()
-    for to in [(blk_y, feat), (blk, feat_x), (blk, feat_c)] + [
-            (place(i, 0), feat) for i in range(1, nz)]:
+
+    def greet(to):
         pl.semaphore_signal(barrier, inc=1, device_id=to, device_id_type=MESH)
+
+    for to in ((blk_y, feat), (blk, feat_x), (blk, feat_c)):
+        greet(to)
+    along_z(greet)
 
     for t in (0, 1):
         loads[t].wait()
@@ -121,7 +135,7 @@
             n = min(GROUP, rows - q * GROUP)
             buf[t, blk, feat, rows:rows + n, q * rem:(q + 1) * rem] = last[q * GROUP:q * GROUP + n]
 
-    pl.semaphore_wait(barrier, 3 + nz - 1)
+    pl.semaphore_wait(barrier, 3 + jnp.where(has_up, 1, 0) + jnp.where(has_down, 1, 0))
 
     sent = []
 
@@ -161,10 +175,13 @@
         b, f = place(i, dy), feat_x if dx else feat
         if came >= 0:
             arrive(h, t, b, f)
+        if i and order[came] == "z":
+            send(h, t, b, f, (blk + 2, feat), jnp.logical_and(planes[i] < z, has_up))
+            send(h, t, b, f, (blk - 2, feat), jnp.logical_and(planes[i] > z, has_down))
         for axis in order[came + 1:]:
             if axis == "z":
-                for other in range(1, nz):
-                    send(h, t, b, f, (planes[other] * 2 + y, feat))
+                send(h, t, b, f, (blk + 2, feat), has_up)
+                send(h, t, b, f, (blk - 2, feat), has_down)
             else:
                 send(h, t, b, f, (blk, feat_x) if axis == "x" else (blk_y, feat))
         send(h, t, b, f, (blk, feat_c), None if i == 0 and dy == 0 else c == t)

time: 56.9 us -> 48.9 us (0.86)
  the two profiles are of different devices: /device:TPU:21 before, /device:TPU:0 now
where the time goes in v4:
time: 48.9 us; the launch traced here: 48.5 us
  Pallas kernels  43.4 us (89%)
  local copies, waits for them, and re-layouts  3.22 us (7%)
  between operations  1.94 us (4%)
    pallas_call x1, Pallas kernels, gathered(): pl.pallas_call(functools.partial(kernel, nz, rows, wide, rem), out_shape=...  43.4 us
    unnamed x6, local copies, waits for them, and re-layouts  3.22 us

profile of v4, /device:TPU:0, one launch (start us, length us, event | category | flops | bytes accessed | tf_op | source)
XLA Modules:
  0.0 48.5 jit_solution(3418190193654589944)
XLA Ops:
  1.9 0.0 copy-start
  1.9 0.9 %copy-done = bf16[176,288]{1,0:T(8,128)(2,1)S(1)} copy-done((bf16[176,288]{1,0:T(8,128)(2,1)S(1)}, bf16[176,288]{1,0:T(8,128)(2,1)}, u32[]{:S(2)}) %copy-start) | copy-done | bytes 101400
  2.8 0.0 copy-start.1
  2.8 0.9 %copy-done.1 = bf16[176,288]{1,0:T(8,128)(2,1)S(1)} copy-done((bf16[176,288]{1,0:T(8,128)(2,1)S(1)}, bf16[176,288]{1,0:T(8,128)(2,1)}, u32[]{:S(2)}) %copy-start.1) | copy-done | bytes 101400
  3.7 43.4 %shard_map.59 = (f32[176,288]{1,0:T(8,128)S(1)}, f32[176,288]{1,0:T(8,128)S(1)}) custom-call(bf16[176,288]{1,0:T(8,128)(2,1)S(1)} %copy-done, bf16[176,288]{1,0:T(8,128)(2,1)S(1)} %copy-done.1, f32[1]{0:T(128)} %bitcast.2.scale_ref, f32[1]{0:T(128)} %bitcast.3.bias_ref), custom_call_target="tpu_custom_call" | custom-call | tf_op jit(solution)/shard_map/pallas_call | solution.py:274
  47.1 0.7 %copy.10 = f32[176,288]{1,0:T(8,128)} copy(f32[176,288]{1,0:T(8,128)S(1)} %get-tuple-element.4) | data formatting | bytes 405504
  47.8 0.7 %copy.11 = f32[176,288]{1,0:T(8,128)} copy(f32[176,288]{1,0:T(8,128)S(1)} %get-tuple-element.5) | data formatting | bytes 405504
Async XLA Ops:
  1.9 0.9 %copy-start = (bf16[176,288]{1,0:T(8,128)(2,1)S(1)}, bf16[176,288]{1,0:T(8,128)(2,1)}, u32[]{:S(2)}) copy-start(bf16[176,288]{1,0:T(8,128)(2,1)} %img_ref.1) | copy-start | bytes 304132
  2.8 0.9 %copy-start.1 = (bf16[176,288]{1,0:T(8,128)(2,1)S(1)}, bf16[176,288]{1,0:T(8,128)(2,1)}, u32[]{:S(2)}) copy-start(bf16[176,288]{1,0:T(8,128)(2,1)} %txt_ref.1) | copy-start | bytes 304132

commit v5 on v4

--- a/solution.py
+++ b/solution.py
@@ -65,6 +65,21 @@
 MESH = pl.DeviceIdType.MESH
 BF16 = jnp.bfloat16
 F32 = jnp.float32
+STEPS = (
+    (
+        0, 16, 32, 2, 17, 48, 1, 4, 34, 33, 20, 50, 8, 49, 19, 18, 52, 35, 22, 36,
+        64, 24, 53, 40, 25, 9, 10, 51, 56, 21, 38, 27, 3, 6, 11, 37, 41, 54, 12, 128,
+        55, 28, 66, 42, 5, 14, 57, 44, 60, 29, 30, 39, 58, 23, 26, 68, 59, 61, 43, 13,
+        7, 72, 45, 46, 130, 15, 31, 74, 62, 76, 63, 47, 70, 136, 138, 78, 140, 132, 134, 142,
+    ),
+    (
+        48, 0, 32, 16, 2, 1, 4, 50, 8, 34, 20, 49, 18, 24, 33, 17, 40, 36, 56, 52,
+        35, 9, 51, 5, 3, 22, 12, 38, 6, 19, 28, 64, 44, 26, 53, 42, 57, 21, 25, 39,
+        58, 37, 60, 54, 66, 10, 41, 61, 55, 14, 68, 7, 46, 23, 72, 59, 27, 43, 13, 45,
+        70, 11, 30, 62, 29, 136, 15, 74, 76, 47, 31, 63, 128, 132, 130, 78, 134, 138, 140, 142,
+    ),
+)
+PLANES = 4
 GROUP = 32
 
 
@@ -89,7 +104,7 @@
     feat_xc = (1 - x) * 2 + 1 - c
     near = jnp.minimum(z, nz - 1 - z)
     groups = -(-rows // GROUP)
-    cut = (rows + GROUP) * 2 // 5 // 16 * 16
+    cut = (rows + GROUP) * 5 // 13 // 16 * 16
     has_up, has_down = z < nz - 1, z > 0
     ranges = ((0, cut), (cut, rows + GROUP - cut))
     orders = (("zyx", "zxy"), ("yzx", "xzy"))
@@ -211,8 +226,6 @@
                     arrive(h, c, b, f)
         if i == 0 and dy == 0:
             unpack(mine, c, b)
-            acc[...] = jnp.zeros_like(acc)
-            accr[...] = jnp.zeros_like(accr)
         unpack(theirs, u, b)
         dots = dot_nt(mine[...], theirs[...])
         for f in range(4):
@@ -245,18 +258,28 @@
             acc[t] += jnp.dot(slope, buf[1 - t, b, feat, 0:rows, :], preferred_element_type=F32)
             accr[t] += jnp.dot(slope, own_rem[1 - t], preferred_element_type=F32)
 
-    events = []
-    for i in range(nz):
-        for dy in (0, 1):
-            for dx in (0, 1):
-                for h in (0, 1):
-                    for t in (0, 1):
-                        events.append((i + dy + dx, len(events), relay, (h, t, i, dy, dx)))
-            events.append((i + dy + 2.5, len(events), finish, (i, dy)))
-            events.append((i + dy + 3.6, len(events), apply, (i, dy)))
-    events.append((nz + 2.4, len(events), wait_sent, ()))
-    for _, _, run, args in sorted(events, key=lambda event: event[:2]):
-        run(*args)
+    acc[...] = jnp.zeros_like(acc)
+    accr[...] = jnp.zeros_like(accr)
+
+    def steps(codes):
+        sent.clear()
+        slopes = 0
+        for step in codes:
+            kind, part, i, dy, dx = step // 64, step // 16 % 4, step // 4 % 4, step // 2 % 2, step % 2
+            if kind == 0:
+                relay(part // 2, part % 2, i, dy, dx)
+            elif kind == 1:
+                finish(i, dy)
+                slopes += 1
+                if slopes == 2 * nz:
+                    wait_sent()
+            else:
+                apply(i, dy)
+
+    for inner, codes in enumerate(STEPS):
+        @pl.when((near > 0) == bool(inner))
+        def _():
+            steps(codes)
 
     for t, ref in ((0, gi_ref), (1, gt_ref)):
         ref[:, 0:wide] = scale * acc[t]
@@ -305,7 +328,7 @@
 
     def body(image, text, scale, bias):
         whole = 2 * blocks * feats * image.size * 2
-        if feats == 4 and blocks % 2 == 0 and whole <= 16 * 2**20:
+        if feats == 4 and blocks == 2 * PLANES and whole <= 16 * 2**20:
             return gathered(blocks, image, text, scale, bias)
         return shards(image, text, scale, bias)
 

time: 48.9 us -> 45.9 us (0.939)
  Pallas kernels: 43.4 us -> 40.6 us
    pallas_call x1, Pallas kernels: 43.4 us -> 40.6 us  [gathered(): pl.pallas_call(functools.partial(kernel, nz, rows, wide, rem), out_shape=...]
where the time goes in v5:
time: 45.9 us; the launch traced here: 45.8 us
  Pallas kernels  40.6 us (88%)
  local copies, waits for them, and re-layouts  3.22 us (7%)
  between operations  1.94 us (4%)
    pallas_call x1, Pallas kernels, gathered(): pl.pallas_call(functools.partial(kernel, nz, rows, wide, rem), out_shape=...  40.6 us
    unnamed x6, local copies, waits for them, and re-layouts  3.22 us

profile of v5, /device:TPU:0, one launch (start us, length us, event | category | flops | bytes accessed | tf_op | source)
XLA Modules:
  0.0 45.8 jit_solution(7948636691057488416)
XLA Ops:
  1.9 0.0 copy-start
  1.9 0.9 %copy-done = bf16[176,288]{1,0:T(8,128)(2,1)S(1)} copy-done((bf16[176,288]{1,0:T(8,128)(2,1)S(1)}, bf16[176,288]{1,0:T(8,128)(2,1)}, u32[]{:S(2)}) %copy-start) | copy-done | bytes 101400
  2.8 0.0 copy-start.1
  2.8 0.9 %copy-done.1 = bf16[176,288]{1,0:T(8,128)(2,1)S(1)} copy-done((bf16[176,288]{1,0:T(8,128)(2,1)S(1)}, bf16[176,288]{1,0:T(8,128)(2,1)}, u32[]{:S(2)}) %copy-start.1) | copy-done | bytes 101400
  3.7 40.6 %shard_map.59 = (f32[176,288]{1,0:T(8,128)S(1)}, f32[176,288]{1,0:T(8,128)S(1)}) custom-call(bf16[176,288]{1,0:T(8,128)(2,1)S(1)} %copy-done, bf16[176,288]{1,0:T(8,128)(2,1)S(1)} %copy-done.1, f32[1]{0:T(128)} %bitcast.2.scale_ref, f32[1]{0:T(128)} %bitcast.3.bias_ref), custom_call_target="tpu_custom_call" | custom-call | tf_op jit(solution)/shard_map/pallas_call | solution.py:297
  44.4 0.7 %copy.10 = f32[176,288]{1,0:T(8,128)} copy(f32[176,288]{1,0:T(8,128)S(1)} %get-tuple-element.4) | data formatting | bytes 405504
  45.1 0.7 %copy.11 = f32[176,288]{1,0:T(8,128)} copy(f32[176,288]{1,0:T(8,128)S(1)} %get-tuple-element.5) | data formatting | bytes 405504
Async XLA Ops:
  1.9 0.9 %copy-start = (bf16[176,288]{1,0:T(8,128)(2,1)S(1)}, bf16[176,288]{1,0:T(8,128)(2,1)}, u32[]{:S(2)}) copy-start(bf16[176,288]{1,0:T(8,128)(2,1)} %img_ref.1) | copy-start | bytes 304132
  2.8 0.9 %copy-start.1 = (bf16[176,288]{1,0:T(8,128)(2,1)S(1)}, bf16[176,288]{1,0:T(8,128)(2,1)}, u32[]{:S(2)}) copy-start(bf16[176,288]{1,0:T(8,128)(2,1)} %txt_ref.1) | copy-start | bytes 304132

commit v6 on v5

--- a/solution.py
+++ b/solution.py
@@ -67,16 +67,16 @@
 F32 = jnp.float32
 STEPS = (
     (
-        0, 16, 32, 2, 17, 48, 1, 4, 34, 33, 20, 50, 8, 49, 19, 18, 52, 35, 22, 36,
-        64, 24, 53, 40, 25, 9, 10, 51, 56, 21, 38, 27, 3, 6, 11, 37, 41, 54, 12, 128,
-        55, 28, 66, 42, 5, 14, 57, 44, 60, 29, 30, 39, 58, 23, 26, 68, 59, 61, 43, 13,
-        7, 72, 45, 46, 130, 15, 31, 74, 62, 76, 63, 47, 70, 136, 138, 78, 140, 132, 134, 142,
+        16, 48, 0, 32, 17, 1, 2, 4, 49, 34, 19, 5, 6, 20, 35, 52, 8, 18, 51, 38,
+        33, 36, 24, 3, 56, 50, 40, 37, 9, 21, 54, 58, 10, 42, 7, 53, 64, 12, 68, 11,
+        25, 28, 26, 57, 39, 41, 44, 43, 55, 66, 22, 23, 60, 14, 72, 29, 130, 13, 30, 27,
+        45, 46, 59, 15, 61, 132, 70, 74, 62, 128, 47, 63, 31, 134, 76, 78, 136, 140, 138, 142,
     ),
     (
-        48, 0, 32, 16, 2, 1, 4, 50, 8, 34, 20, 49, 18, 24, 33, 17, 40, 36, 56, 52,
-        35, 9, 51, 5, 3, 22, 12, 38, 6, 19, 28, 64, 44, 26, 53, 42, 57, 21, 25, 39,
-        58, 37, 60, 54, 66, 10, 41, 61, 55, 14, 68, 7, 46, 23, 72, 59, 27, 43, 13, 45,
-        70, 11, 30, 62, 29, 136, 15, 74, 76, 47, 31, 63, 128, 132, 130, 78, 134, 138, 140, 142,
+        48, 32, 0, 16, 34, 49, 8, 2, 18, 4, 33, 1, 24, 56, 50, 20, 40, 52, 35, 5,
+        36, 17, 10, 6, 3, 9, 58, 51, 38, 28, 42, 64, 54, 12, 53, 25, 44, 37, 57, 7,
+        30, 21, 60, 19, 22, 26, 46, 41, 27, 55, 66, 39, 128, 61, 29, 11, 23, 43, 68, 13,
+        59, 130, 14, 70, 63, 72, 45, 31, 62, 47, 74, 132, 15, 76, 136, 78, 134, 138, 140, 142,
     ),
 )
 PLANES = 4
@@ -316,7 +316,7 @@
             pltpu.SemaphoreType.DMA((blocks,)),
         ],
         compiler_params=pltpu.CompilerParams(
-            collective_id=0, has_side_effects=True, vmem_limit_bytes=48 * 2**20
+            collective_id=0, has_side_effects=True, vmem_limit_bytes=121 * 2**19
         ),
     )(image, text, scale.reshape(1), bias.reshape(1))
 

time: 45.9 us -> 44.9 us (0.978)
  local copies, waits for them, and re-layouts: 3.22 us -> 2.43 us
    unnamed x6 -> x4, local copies, waits for them, and re-layouts: 3.22 us -> 2.43 us
where the time goes in v6:
time: 44.9 us; the launch traced here: 44.7 us
  Pallas kernels  40.4 us (90%)
  local copies, waits for them, and re-layouts  2.43 us (5%)
  between operations  1.94 us (4%)
    pallas_call x1, Pallas kernels, gathered(): pl.pallas_call(functools.partial(kernel, nz, rows, wide, rem), out_shape=...  40.4 us
    unnamed x4, local copies, waits for them, and re-layouts  2.43 us

profile of v6, /device:TPU:0, one launch (start us, length us, event | category | flops | bytes accessed | tf_op | source)
XLA Modules:
  0.0 44.7 jit_solution(4654208812540231989)
XLA Ops:
  1.9 40.4 %shard_map.59 = (f32[176,288]{1,0:T(8,128)}, f32[176,288]{1,0:T(8,128)}) custom-call(bf16[176,288]{1,0:T(8,128)(2,1)} %img_ref.1, bf16[176,288]{1,0:T(8,128)(2,1)} %txt_ref.1, f32[1]{0:T(128)} %bitcast.2.scale_ref, f32[1]{0:T(128)} %bitcast.3.bias_ref), custom_call_target="tpu_custom_call" | custom-call | tf_op jit(solution)/shard_map/pallas_call | solution.py:297
  42.3 0.0 copy-start
  42.3 1.7 %copy.10 = f32[176,288]{1,0:T(8,128)} copy(f32[176,288]{1,0:T(8,128)} %get-tuple-element.4) | data formatting | bytes 405504
  44.0 0.0 copy-done
  44.0 0.7 %copy.11 = f32[176,288]{1,0:T(8,128)} copy(f32[176,288]{1,0:T(8,128)S(1)} %copy-done) | data formatting | bytes 405504
Async XLA Ops:
  42.3 1.7 %copy-start = (f32[176,288]{1,0:T(8,128)S(1)}, f32[176,288]{1,0:T(8,128)}, u32[]{:S(2)}) copy-start(f32[176,288]{1,0:T(8,128)} %get-tuple-element.5) | copy-start | bytes 608260

commit v7 on v6

--- a/solution.py
+++ b/solution.py
@@ -67,16 +67,16 @@
 F32 = jnp.float32
 STEPS = (
     (
-        16, 48, 0, 32, 17, 1, 2, 4, 49, 34, 19, 5, 6, 20, 35, 52, 8, 18, 51, 38,
-        33, 36, 24, 3, 56, 50, 40, 37, 9, 21, 54, 58, 10, 42, 7, 53, 64, 12, 68, 11,
-        25, 28, 26, 57, 39, 41, 44, 43, 55, 66, 22, 23, 60, 14, 72, 29, 130, 13, 30, 27,
-        45, 46, 59, 15, 61, 132, 70, 74, 62, 128, 47, 63, 31, 134, 76, 78, 136, 140, 138, 142,
+        48, 0, 32, 49, 52, 2, 16, 34, 20, 1, 50, 4, 36, 18, 17, 51, 38, 35, 53, 8,
+        33, 24, 40, 5, 6, 37, 19, 54, 21, 22, 56, 9, 10, 64, 42, 25, 28, 3, 23, 26,
+        68, 58, 55, 41, 39, 12, 44, 7, 57, 66, 11, 43, 27, 60, 29, 132, 14, 46, 72, 59,
+        61, 70, 45, 62, 130, 31, 30, 13, 15, 74, 47, 63, 128, 76, 78, 138, 134, 140, 136, 142,
     ),
     (
-        48, 32, 0, 16, 34, 49, 8, 2, 18, 4, 33, 1, 24, 56, 50, 20, 40, 52, 35, 5,
-        36, 17, 10, 6, 3, 9, 58, 51, 38, 28, 42, 64, 54, 12, 53, 25, 44, 37, 57, 7,
-        30, 21, 60, 19, 22, 26, 46, 41, 27, 55, 66, 39, 128, 61, 29, 11, 23, 43, 68, 13,
-        59, 130, 14, 70, 63, 72, 45, 31, 62, 47, 74, 132, 15, 76, 136, 78, 134, 138, 140, 142,
+        48, 32, 0, 16, 49, 34, 8, 1, 36, 4, 17, 33, 24, 20, 52, 40, 56, 2, 6, 38,
+        51, 18, 19, 42, 28, 35, 44, 64, 37, 21, 9, 12, 53, 50, 3, 57, 41, 128, 60, 25,
+        10, 39, 46, 5, 14, 66, 61, 72, 22, 55, 26, 7, 54, 30, 23, 45, 58, 62, 29, 13,
+        68, 11, 27, 43, 59, 130, 70, 31, 15, 47, 63, 132, 76, 74, 78, 134, 140, 136, 138, 142,
     ),
 )
 PLANES = 4
@@ -316,7 +316,7 @@
             pltpu.SemaphoreType.DMA((blocks,)),
         ],
         compiler_params=pltpu.CompilerParams(
-            collective_id=0, has_side_effects=True, vmem_limit_bytes=121 * 2**19
+            collective_id=0, has_side_effects=True, vmem_limit_bytes=60 * 2**20
         ),
     )(image, text, scale.reshape(1), bias.reshape(1))
 

time: 44.9 us -> 42.2 us (0.940)
  Pallas kernels: 40.4 us -> 37.6 us
    pallas_call x1, Pallas kernels: 40.4 us -> 37.6 us  [gathered(): pl.pallas_call(functools.partial(kernel, nz, rows, wide, rem), out_shape=...]
where the time goes in v7:
time: 42.2 us; the launch traced here: 42 us
  Pallas kernels  37.6 us (89%)
  local copies, waits for them, and re-layouts  2.43 us (6%)
  between operations  1.94 us (5%)
    pallas_call x1, Pallas kernels, gathered(): pl.pallas_call(functools.partial(kernel, nz, rows, wide, rem), out_shape=...  37.6 us
    unnamed x4, local copies, waits for them, and re-layouts  2.43 us

profile of v7, /device:TPU:0, one launch (start us, length us, event | category | flops | bytes accessed | tf_op | source)
XLA Modules:
  0.0 42.0 jit_solution(4189491697731220950)
XLA Ops:
  1.9 37.6 %shard_map.59 = (f32[176,288]{1,0:T(8,128)}, f32[176,288]{1,0:T(8,128)}) custom-call(bf16[176,288]{1,0:T(8,128)(2,1)} %img_ref.1, bf16[176,288]{1,0:T(8,128)(2,1)} %txt_ref.1, f32[1]{0:T(128)} %bitcast.2.scale_ref, f32[1]{0:T(128)} %bitcast.3.bias_ref), custom_call_target="tpu_custom_call" | custom-call | tf_op jit(solution)/shard_map/pallas_call | solution.py:297
  39.6 0.0 copy-start
  39.6 1.7 %copy.10 = f32[176,288]{1,0:T(8,128)} copy(f32[176,288]{1,0:T(8,128)} %get-tuple-element.4) | data formatting | bytes 405504
  41.3 0.0 copy-done
  41.3 0.7 %copy.11 = f32[176,288]{1,0:T(8,128)} copy(f32[176,288]{1,0:T(8,128)S(1)} %copy-done) | data formatting | bytes 405504
Async XLA Ops:
  39.6 1.7 %copy-start = (f32[176,288]{1,0:T(8,128)S(1)}, f32[176,288]{1,0:T(8,128)}, u32[]{:S(2)}) copy-start(f32[176,288]{1,0:T(8,128)} %get-tuple-element.5) | copy-start | bytes 608260

commit v8 on v7

--- a/solution.py
+++ b/solution.py
@@ -67,16 +67,16 @@
 F32 = jnp.float32
 STEPS = (
     (
-        48, 0, 32, 49, 52, 2, 16, 34, 20, 1, 50, 4, 36, 18, 17, 51, 38, 35, 53, 8,
-        33, 24, 40, 5, 6, 37, 19, 54, 21, 22, 56, 9, 10, 64, 42, 25, 28, 3, 23, 26,
-        68, 58, 55, 41, 39, 12, 44, 7, 57, 66, 11, 43, 27, 60, 29, 132, 14, 46, 72, 59,
-        61, 70, 45, 62, 130, 31, 30, 13, 15, 74, 47, 63, 128, 76, 78, 138, 134, 140, 136, 142,
+        48, 0, 32, 16, 2, 36, 49, 4, 34, 52, 20, 50, 18, 1, 38, 17, 8, 3, 53, 33,
+        5, 37, 54, 51, 24, 35, 21, 6, 40, 22, 10, 39, 56, 64, 42, 9, 25, 55, 19, 68,
+        28, 26, 58, 41, 23, 12, 11, 27, 44, 57, 7, 66, 43, 60, 14, 13, 29, 72, 46, 59,
+        61, 70, 130, 31, 45, 15, 74, 30, 63, 62, 47, 128, 134, 76, 78, 138, 132, 136, 140, 142,
     ),
     (
-        48, 32, 0, 16, 49, 34, 8, 1, 36, 4, 17, 33, 24, 20, 52, 40, 56, 2, 6, 38,
-        51, 18, 19, 42, 28, 35, 44, 64, 37, 21, 9, 12, 53, 50, 3, 57, 41, 128, 60, 25,
-        10, 39, 46, 5, 14, 66, 61, 72, 22, 55, 26, 7, 54, 30, 23, 45, 58, 62, 29, 13,
-        68, 11, 27, 43, 59, 130, 70, 31, 15, 47, 63, 132, 76, 74, 78, 134, 140, 136, 138, 142,
+        48, 32, 0, 16, 49, 33, 34, 1, 4, 8, 36, 17, 20, 24, 2, 40, 52, 18, 56, 6,
+        50, 38, 35, 42, 37, 28, 12, 64, 44, 57, 53, 9, 51, 41, 19, 21, 3, 7, 60, 25,
+        5, 10, 128, 39, 46, 61, 66, 23, 14, 29, 55, 72, 58, 54, 45, 22, 11, 62, 68, 27,
+        59, 43, 26, 30, 47, 13, 70, 15, 130, 31, 63, 74, 76, 78, 134, 136, 132, 138, 140, 142,
     ),
 )
 PLANES = 4

time: 42.2 us -> 42.5 us (level)
  no operation moved by 1% of the time
where the time goes in v8:
time: 42.5 us; the launch traced here: 42.4 us
  Pallas kernels  38 us (89%)
  local copies, waits for them, and re-layouts  2.43 us (6%)
  between operations  1.94 us (5%)
    pallas_call x1, Pallas kernels, gathered(): pl.pallas_call(functools.partial(kernel, nz, rows, wide, rem), out_shape=...  38 us
    unnamed x4, local copies, waits for them, and re-layouts  2.43 us

profile of v8, /device:TPU:0, one launch (start us, length us, event | category | flops | bytes accessed | tf_op | source)
XLA Modules:
  0.0 42.4 jit_solution(10496972315137663477)
XLA Ops:
  1.9 38.0 %shard_map.59 = (f32[176,288]{1,0:T(8,128)}, f32[176,288]{1,0:T(8,128)}) custom-call(bf16[176,288]{1,0:T(8,128)(2,1)} %img_ref.1, bf16[176,288]{1,0:T(8,128)(2,1)} %txt_ref.1, f32[1]{0:T(128)} %bitcast.2.scale_ref, f32[1]{0:T(128)} %bitcast.3.bias_ref), custom_call_target="tpu_custom_call" | custom-call | tf_op jit(solution)/shard_map/pallas_call | solution.py:297
  39.9 0.0 copy-start
  39.9 1.7 %copy.10 = f32[176,288]{1,0:T(8,128)} copy(f32[176,288]{1,0:T(8,128)} %get-tuple-element.4) | data formatting | bytes 405504
  41.6 0.0 copy-done
  41.6 0.7 %copy.11 = f32[176,288]{1,0:T(8,128)} copy(f32[176,288]{1,0:T(8,128)S(1)} %copy-done) | data formatting | bytes 405504
Async XLA Ops:
  39.9 1.7 %copy-start = (f32[176,288]{1,0:T(8,128)S(1)}, f32[176,288]{1,0:T(8,128)}, u32[]{:S(2)}) copy-start(f32[176,288]{1,0:T(8,128)} %get-tuple-element.5) | copy-start | bytes 608260

commit v9 on v7

--- a/solution.py
+++ b/solution.py
@@ -282,8 +282,8 @@
             steps(codes)
 
     for t, ref in ((0, gi_ref), (1, gt_ref)):
-        ref[:, 0:wide] = scale * acc[t]
-        ref[:, wide:wide + rem] = scale * accr[t]
+        ref[:, 0:wide] = acc[t]
+        ref[:, wide:wide + rem] = accr[t]
     for b in range(nz * 2):
         hand(b).wait_send()
 
@@ -294,7 +294,7 @@
     rem = width - wide
     nz = blocks // 2
     out = jax.ShapeDtypeStruct((rows, width), F32)
-    return pl.pallas_call(
+    image_sum, text_sum = pl.pallas_call(
         functools.partial(kernel, nz, rows, wide, rem),
         out_shape=(out, out),
         in_specs=[pl.BlockSpec(memory_space=pl.ANY)] * 2
@@ -319,6 +319,7 @@
             collective_id=0, has_side_effects=True, vmem_limit_bytes=60 * 2**20
         ),
     )(image, text, scale.reshape(1), bias.reshape(1))
+    return scale * image_sum, scale * text_sum
 
 
 def solution(mesh):

time: 42.2 us -> 41.6 us (0.986)
  local copies, waits for them, and re-layouts: 2.43 us -> 0 us
  other arithmetic: 0 us -> 1.87 us
    unnamed x4 -> x0, local copies, waits for them, and re-layouts: 2.43 us -> none
    mul x0 -> x1, other arithmetic: none -> 1.87 us  [gathered(): return (scale * image_sum, scale * text_sum)]
where the time goes in v9:
time: 41.6 us; the launch traced here: 41.4 us
  Pallas kernels  37.6 us (90%)
  between operations  1.93 us (5%)
  other arithmetic  1.87 us (4%)
    pallas_call x1, Pallas kernels, gathered(): pl.pallas_call(functools.partial(kernel, nz, rows, wide, rem), out_shape=...  37.6 us
    mul x1, other arithmetic, gathered(): return (scale * image_sum, scale * text_sum)  1.87 us

profile of v9, /device:TPU:0, one launch (start us, length us, event | category | flops | bytes accessed | tf_op | source)
XLA Modules:
  0.0 41.4 jit_solution(10321459870795668659)
XLA Ops:
  1.9 37.6 %shard_map.59 = (f32[176,288]{1,0:T(8,128)}, f32[176,288]{1,0:T(8,128)}) custom-call(bf16[176,288]{1,0:T(8,128)(2,1)} %img_ref.1, bf16[176,288]{1,0:T(8,128)(2,1)} %txt_ref.1, f32[1]{0:T(128)} %bitcast.2.scale_ref, f32[1]{0:T(128)} %bitcast.3.bias_ref), custom_call_target="tpu_custom_call" | custom-call | tf_op jit(solution)/shard_map/pallas_call | solution.py:297
  39.6 1.9 %broadcast_multiply_fusion = (f32[176,288]{1,0:T(8,128)}, f32[176,288]{1,0:T(8,128)}) fusion(f32[176,288]{1,0:T(8,128)} %get-tuple-element.5, f32[]{:T(128)} %copy.6, f32[176,288]{1,0:T(8,128)} %get-tuple-element.4), kind=kLoop, calls=%fused_computation | loop fusion | flops 101376 | bytes 811012 | tf_op jit(solution)/shard_map/mul | solution.py:322

commit v10 on v9

--- a/solution.py
+++ b/solution.py
@@ -73,10 +73,10 @@
         61, 70, 45, 62, 130, 31, 30, 13, 15, 74, 47, 63, 128, 76, 78, 138, 134, 140, 136, 142,
     ),
     (
-        48, 32, 0, 16, 49, 34, 8, 1, 36, 4, 17, 33, 24, 20, 52, 40, 56, 2, 6, 38,
-        51, 18, 19, 42, 28, 35, 44, 64, 37, 21, 9, 12, 53, 50, 3, 57, 41, 128, 60, 25,
-        10, 39, 46, 5, 14, 66, 61, 72, 22, 55, 26, 7, 54, 30, 23, 45, 58, 62, 29, 13,
-        68, 11, 27, 43, 59, 130, 70, 31, 15, 47, 63, 132, 76, 74, 78, 134, 140, 136, 138, 142,
+        48, 32, 0, 16, 49, 33, 34, 1, 4, 8, 36, 17, 20, 24, 2, 40, 52, 18, 56, 6,
+        50, 38, 35, 42, 37, 28, 12, 64, 44, 57, 53, 9, 51, 41, 19, 21, 3, 7, 60, 25,
+        5, 10, 128, 39, 46, 61, 66, 23, 14, 29, 55, 72, 58, 54, 45, 22, 11, 62, 68, 27,
+        59, 43, 26, 30, 47, 13, 70, 15, 130, 31, 63, 74, 76, 78, 134, 136, 132, 138, 140, 142,
     ),
 )
 PLANES = 4

time: 41.6 us -> 41.7 us (level)
  no operation moved by 1% of the time
where the time goes in v10:
time: 41.7 us; the launch traced here: 41.5 us
  Pallas kernels  37.7 us (90%)
  between operations  1.93 us (5%)
  other arithmetic  1.87 us (4%)
    pallas_call x1, Pallas kernels, gathered(): pl.pallas_call(functools.partial(kernel, nz, rows, wide, rem), out_shape=...  37.7 us
    mul x1, other arithmetic, gathered(): return (scale * image_sum, scale * text_sum)  1.87 us

profile of v10, /device:TPU:0, one launch (start us, length us, event | category | flops | bytes accessed | tf_op | source)
XLA Modules:
  0.0 41.5 jit_solution(16951525117757749269)
XLA Ops:
  1.9 37.7 %shard_map.59 = (f32[176,288]{1,0:T(8,128)}, f32[176,288]{1,0:T(8,128)}) custom-call(bf16[176,288]{1,0:T(8,128)(2,1)} %img_ref.1, bf16[176,288]{1,0:T(8,128)(2,1)} %txt_ref.1, f32[1]{0:T(128)} %bitcast.2.scale_ref, f32[1]{0:T(128)} %bitcast.3.bias_ref), custom_call_target="tpu_custom_call" | custom-call | tf_op jit(solution)/shard_map/pallas_call | solution.py:297
  39.7 1.9 %broadcast_multiply_fusion = (f32[176,288]{1,0:T(8,128)}, f32[176,288]{1,0:T(8,128)}) fusion(f32[176,288]{1,0:T(8,128)} %get-tuple-element.5, f32[]{:T(128)} %copy.6, f32[176,288]{1,0:T(8,128)} %get-tuple-element.4), kind=kLoop, calls=%fused_computation | loop fusion | flops 101376 | bytes 811012 | tf_op jit(solution)/shard_map/mul | solution.py:322
